TPU v7x, 256 devices: a whole 4x4x8 slice. The times are simulated.
256 devices in a mesh: dp: 32 (over x, z), fsdp: 8 (over y, core).
Axes of the slice: x: 4, y: 4, z: 8, core: 2. Of those that a mesh axis runs over, the one named last changes fastest.
Arguments:
- inputs: bfloat16 [24576, 1152], P('dp'), may hold values from -6 to 6
- cotangent: bfloat16 [24576, 1152], P('dp')
- gate_weight: bfloat16 [1152, 6912], P(None, 'fsdp'), may hold values from -0.1875 to 0.1875
- up_weight: bfloat16 [1152, 6912], P(None, 'fsdp')
- down_weight: bfloat16 [6912, 1152], P('fsdp'), may hold values from -0.078125 to 0.078125
- live_counts: int32 [32], P('dp'), may hold values from 1 to 3, as said below
- noise_gate: float32 [1152, 6912], P('dp', 'fsdp'), may hold values from -6 to 6
- noise_up: float32 [1152, 6912], P('dp', 'fsdp'), may hold values from -6 to 6
- noise_down: float32 [6912, 1152], P('fsdp', 'dp'), may hold values from -6 to 6
Outputs:
- grad_gate: float32 [1152, 6912], P('dp', 'fsdp')
- grad_up: float32 [1152, 6912], P('dp', 'fsdp')
- grad_down: float32 [6912, 1152], P('fsdp', 'dp')
Inputs may be any that keep to these rules, and one draw needn't show every extreme that they name: The first live_counts[d] slots of data-parallel index d hold its sampled sequences; the others are unused.
All inputs are finite; a program needn't handle non-finite values.
Results may differ from a plain program's by a relative error of at most 0.0038.
Values may be sent and summed in bfloat16 or wider, within the bound.
A program may use at most 128 MiB of HBM per device.

v0:
```python
import math

import jax
import jax.numpy as jnp
from jax import lax
from jax.sharding import PartitionSpec as P

D = 1152
FF = 6912
SEQ = 256
SLOTS = 3


gelu_scale = 0.7978845608028654
gelu_cube = 0.044715


def gelu_pair(values):
    tanh_arg = gelu_scale * (values + gelu_cube * values * values * values)
    tangent = jnp.tanh(tanh_arg)
    gelu_value = 0.5 * values * (1.0 + tangent)
    gelu_slope = 0.5 * (1.0 + tangent) + 0.5 * values * (1.0 - tangent * tangent) * gelu_scale * (
        1.0 + 3.0 * gelu_cube * values * values
    )
    return (gelu_value, gelu_slope)


def outer_rows(left_side, right_side):
    return lax.dot_general(
        left_side, right_side, (((0,), (0,)), ((), ())), preferred_element_type=jnp.float32
    )


def inner_rows(left_side, right_side):
    return lax.dot_general(
        left_side, right_side, (((1,), (1,)), ((), ())), preferred_element_type=jnp.float32
    )


def slot_terms(rows_now, grad_now, gate_weight, up_weight, down_weight):
    gate_pre = jnp.dot(rows_now, gate_weight, preferred_element_type=jnp.float32)
    up_pre = jnp.dot(rows_now, up_weight, preferred_element_type=jnp.float32)
    gelu_value, gelu_slope = gelu_pair(gate_pre)
    hidden = (gelu_value * up_pre).astype(jnp.bfloat16)
    back_grad = inner_rows(grad_now, down_weight)
    d_gate = (back_grad * up_pre * gelu_slope).astype(jnp.bfloat16)
    d_up = (back_grad * gelu_value).astype(jnp.bfloat16)
    grad_gate = outer_rows(rows_now, d_gate)
    grad_up = outer_rows(rows_now, d_up)
    grad_down = outer_rows(hidden, grad_now)
    partial_value = (
        jnp.sum(grad_gate * grad_gate) + jnp.sum(grad_up * grad_up) + jnp.sum(grad_down * grad_down)
    )
    return (hidden, d_gate, d_up, partial_value)


def per_device(
    inputs,
    cotangent,
    gate_weight,
    up_weight,
    down_weight,
    live_counts,
    noise_gate,
    noise_up,
    noise_down,
):
    feature_width = inputs.shape[1]
    hidden_local = gate_weight.shape[1]
    slot_total = SLOTS
    seq_len = SEQ
    bound = 0.1 * math.sqrt(SEQ * D * FF)
    slot_rows = inputs.reshape(slot_total, seq_len, feature_width)
    slot_grad = cotangent.reshape(slot_total, seq_len, feature_width)
    live_count = live_counts[0]
    buffers = (
        jnp.zeros((slot_total, seq_len, hidden_local), jnp.bfloat16),
        jnp.zeros((slot_total, seq_len, 2 * hidden_local), jnp.bfloat16),
        jnp.zeros((slot_total, seq_len, feature_width), jnp.bfloat16),
    )
    for slot_index in range(slot_total):
        is_live = (slot_index < live_count).astype(jnp.float32)
        run_hidden_buf, run_mix_buf, run_out_buf = buffers
        rows_now = lax.dynamic_index_in_dim(slot_rows, slot_index, 0, keepdims=False)
        grad_now = lax.dynamic_index_in_dim(slot_grad, slot_index, 0, keepdims=False)
        hidden, d_gate, d_up, partial_value = slot_terms(
            rows_now, grad_now, gate_weight, up_weight, down_weight
        )
        squared = lax.psum(partial_value, "fsdp")
        grad_norm = jnp.sqrt(jnp.maximum(squared, 0.0))
        factor = is_live * bound / jnp.maximum(grad_norm, bound)
        scaled_gate = (d_gate.astype(jnp.float32) * factor).astype(jnp.bfloat16)
        scaled_up = (d_up.astype(jnp.float32) * factor).astype(jnp.bfloat16)
        scaled_out = (grad_now.astype(jnp.float32) * factor).astype(jnp.bfloat16)
        mixed = jnp.concatenate([scaled_gate, scaled_up], axis=1)
        run_hidden_buf = lax.dynamic_update_index_in_dim(run_hidden_buf, hidden, slot_index, 0)
        run_mix_buf = lax.dynamic_update_index_in_dim(run_mix_buf, mixed, slot_index, 0)
        run_out_buf = lax.dynamic_update_index_in_dim(run_out_buf, scaled_out, slot_index, 0)
        buffers = (run_hidden_buf, run_mix_buf, run_out_buf)
    hidden_buf, mix_buf, out_buf = buffers
    flat_rows = slot_rows.reshape(slot_total * seq_len, feature_width)
    flat_hidden = hidden_buf.reshape(slot_total * seq_len, hidden_local)
    flat_mix = mix_buf.reshape(slot_total * seq_len, 2 * hidden_local)
    flat_out = out_buf.reshape(slot_total * seq_len, feature_width)
    gate_block = outer_rows(flat_rows, flat_mix)
    down_block = outer_rows(flat_out, flat_hidden)
    my_share = lax.psum_scatter(
        jnp.concatenate([gate_block, down_block], axis=1), "dp", scatter_dimension=0, tiled=True
    )
    grad_gate = my_share[:, :hidden_local] + noise_gate
    grad_up = my_share[:, hidden_local : 2 * hidden_local] + noise_up
    grad_down = my_share[:, 2 * hidden_local :].T + noise_down
    return (grad_gate, grad_up, grad_down)


def solution(mesh):
    in_specs = (
        P("dp", None),
        P("dp", None),
        P(None, "fsdp"),
        P(None, "fsdp"),
        P("fsdp", None),
        P("dp"),
        P("dp", "fsdp"),
        P("dp", "fsdp"),
        P("fsdp", "dp"),
    )
    out_specs = (P("dp", "fsdp"), P("dp", "fsdp"), P("fsdp", "dp"))
    return jax.shard_map(
        per_device, mesh=mesh, in_specs=in_specs, out_specs=out_specs, check_vma=False
    )
```

profile of v0, /device:TPU:2, one launch (start us, length us, event | category | flops | bytes accessed | tf_op | source)
XLA Modules:
  0.0 360.3 jit_solution(11235911393868582766)
XLA Ops:
  7.2 2.7 fusion.61
  9.9 2.0 fusion.55
  14.3 1.2 multiply_convert_fusion.14
  15.6 1.8 fusion.2
  19.1 1.2 multiply_convert_fusion.6
  20.3 1.9 fusion.6
  22.2 1.8 fusion.7
  24.0 1.8 fusion.8
  25.8 1.2 multiply_convert_fusion.10
  27.0 1.9 fusion.3
  28.9 1.9 fusion.4
  30.9 1.9 fusion.5
  32.7 1.8 fusion
  34.5 1.8 fusion.1
  42.0 15.4 %all-reduce.4 = (f32[]{:T(128)}, f32[]{:T(128)}, f32[]{:T(128)}) all-reduce(f32[]{:T(128)S(6)} %add.104, f32[]{:T(128)S(6)} %add.110, f32[]{:T(128)S(6)} %add.116), channel_id=1, replica_groups=mesh['dp'=32,'fsdp'=8] {'fsdp'}, use_global_device_ids=true, to_apply=%region_3.4 | all-reduce | flops 3 | bytes 24 | tf_op jit(solution)/shard_map/psum | solution.py:89
  59.0 1.2 fusion.32
  60.3 1.7 dynamic_update_slice.30
  63.9 1.0 fusion.30
  64.8 1.0 fusion.31
  65.8 4.7 %copy.25 = bf16[3,256,1728]{2,1,0:T(8,128)(2,1)} copy(bf16[3,256,1728]{1,2,0:T(8,128)(2,1)} %fusion.31) | data formatting | bytes 5308416 | tf_op jit(solution)/shard_map/jit(dynamic_update_index_in_dim)/dynamic_update_slice | solution.py:97
  70.5 5.5 %convolution_bitcast_fusion = f32[1152,1728]{0,1:T(8,128)S(1)} fusion(bf16[768,1728]{1,0:T(8,128)(2,1)} %bitcast.62, bf16[768,1152]{1,0:T(8,128)(2,1)S(1)} %copy-done.4), kind=kOutput, calls=%fused_computation.1 | convolution fusion | flops 3057647616 | bytes 12386304 | tf_op jit(solution)/shard_map/dot_general | solution.py:29
  76.2 1.3 copy-done.6
  77.8 1.0 copy-done.8
  78.8 1.9 convolution_bitcast_fusion.1
  80.7 4.7 %pad_maximum_fusion = f32[1152,2592]{0,1:T(8,128)} fusion(f32[1152,864]{0,1:T(8,128)S(1)} %convolution_bitcast_fusion.1, f32[1152,1728]{0,1:T(8,128)S(1)} %convolution_bitcast_fusion), kind=kLoop, calls=%fused_computation | loop fusion | flops 2985984 | bytes 23887872 | tf_op jit(solution)/shard_map/concatenate | solution.py:108
  85.5 0.9 copy-done.15
  88.2 256.5 %all-reduce.7.cloned.1.call-done = f32[1152,2592]{0,1:T(8,128)} async-done(((f32[1152,2592]{0,1:T(8,128)}), f32[1152,2592]{0,1:T(8,128)}) %all-reduce.7.cloned.1.call-update) | async-done | bytes 11943952
  344.7 2.8 dynamic-slice_add_fusion
  347.5 1.9 copy.29
  349.4 1.9 copy.30
  351.2 1.4 fusion.46
  352.6 0.8 copy.31
  (55 shorter events, 6.5 us)
Async XLA Ops:
  7.2 5.5 %copy-start = (bf16[1152,864]{0,1:T(8,128)(2,1)S(1)}, bf16[1152,864]{0,1:T(8,128)(2,1)}, u32[]{:S(2)}) copy-start(bf16[1152,864]{0,1:T(8,128)(2,1)} %param.12) | copy-start | bytes 5971972
  7.2 337.5 %all-reduce.7.cloned.1.call-start = ((), (), s32[]{:S(2)}) async-start(), calls=%async_computation | async-start | bytes 23887872
  7.2 2.7 copy-start.2
  9.9 2.0 copy-start.3
  11.9 1.6 copy-start.18
  12.7 1.6 copy-start.5
  15.6 17.2 %copy-start.9 = (bf16[256,864]{0,1:T(8,128)(2,1)}, bf16[256,864]{0,1:T(8,128)(2,1)S(1)}, u32[]{:S(2)}) copy-start(bf16[256,864]{0,1:T(8,128)(2,1)S(1)} %get-tuple-element.26) | copy-start | bytes 1327108
  19.1 1.2 copy-start.7
  27.0 1.9 copy-start.13
  27.0 1.9 copy-start.11
  34.5 24.3 %copy-start.10 = (bf16[256,864]{0,1:T(8,128)(2,1)S(1)}, bf16[256,864]{0,1:T(8,128)(2,1)}, u32[]{:S(2)}) copy-start(bf16[256,864]{0,1:T(8,128)(2,1)} %copy-done.9) | copy-start | bytes 1327108
  60.2 2.5 copy-start.12
  60.3 2.5 copy-start.14
  65.8 4.7 %copy-start.4 = (bf16[768,1152]{1,0:T(8,128)(2,1)S(1)}, bf16[768,1152]{1,0:T(8,128)(2,1)}, u32[]{:S(2)}) copy-start(bf16[768,1152]{1,0:T(8,128)(2,1)} %param.9) | copy-start | bytes 5308420
  76.0 1.5 copy-start.6
  77.5 1.3 copy-start.8
  85.4 0.9 copy-start.15
  85.4 1.1 copy-start.16
  85.4 1.3 copy-start.17
  85.5 1.5 copy-start.19
  344.7 8.8 %copy-start.1 = (bf16[1152,864]{0,1:T(8,128)(2,1)S(1)}, bf16[1152,864]{0,1:T(8,128)(2,1)}, u32[]{:S(2)}) copy-start(bf16[1152,864]{0,1:T(8,128)(2,1)} %param.12) | copy-start | bytes 5971972
Sparse Core Ops, SparseCore 0:
  85.6 259.0 all-reduce.6
where the time goes:
time: 361 us; the launch traced here: 360 us
  waiting for transfers between devices  257 us (71%)
  matrix products  35.4 us (10%)
  between operations  23.6 us (7%)
  local copies, waits for them, and re-layouts  16.5 us (5%)
  blocking collectives  15.4 us (4%)
  other arithmetic  12.9 us (4%)
    unnamed x2, waiting for transfers between devices  257 us
    dot_general x11, matrix products, outer_rows(): lax.dot_general(left_side, right_side, (((0,), (0,)), ((), ())), preferre...  23.9 us
    psum x1, blocking collectives, per_device(): squared = lax.psum(partial_value, 'fsdp')  15.4 us
    unnamed x47, local copies, waits for them, and re-layouts  9.89 us
  transfers between devices with their start and end apart: 1, of which 1 were waited for; matrix products, arithmetic and copies ran while one was open for 0% of the time, Pallas kernels for 0%

commit v1 on v0

v1 whole, which is shorter than its diff:
```python
import functools
import math

import jax
import jax.numpy as jnp
from jax import lax
from jax.experimental import pallas as pl
from jax.experimental.pallas import tpu as pltpu
from jax.sharding import PartitionSpec as P

D = 1152
FF = 6912
SEQ = 256
SLOTS = 3
NX = 4
NZ = 8
OWN = D // (NX * NZ)
XROWS = D // NX
ZROWS = D // NZ
LANE = 128
F32 = jnp.float32
BF16 = jnp.bfloat16
MESH = pl.DeviceIdType.MESH

gelu_scale = 0.7978845608028654
gelu_cube = 0.044715

HP = 896
UP_A = 512
WA = HP + UP_A
WU_B = HP - UP_A
WB = WU_B + HP
A_HALF = ((0, 768), (768, 1408))
B_HALF = ((0, 640), (640, 1280))
A2_TILES = (5, 6)
B2_TILES = (5, 5)


def pad16(n):
    return (n + 15) // 16 * 16


A2_ROWS = tuple(pad16(OWN * t) for t in A2_TILES)
B2_ROWS = tuple(pad16(OWN * t) for t in B2_TILES)


def gelu_pair(values):
    square = values * values
    tangent = jnp.tanh(values * (gelu_scale + (gelu_scale * gelu_cube) * square))
    half_sum = 0.5 + 0.5 * tangent
    gelu_value = values * half_sum
    gelu_slope = half_sum + (0.5 * values) * (1.0 - tangent * tangent) * (
        gelu_scale + (3.0 * gelu_scale * gelu_cube) * square
    )
    return gelu_value, gelu_slope


def nt(a, b):
    return lax.dot_general(a, b, (((1,), (1,)), ((), ())), preferred_element_type=F32)


def nn(a, b):
    return lax.dot_general(a, b, (((1,), (0,)), ((), ())), preferred_element_type=F32)


def kernel(
    n_f, seq, hidden, bound,
    live_ref, x_hbm, c_hbm, wg_hbm, wu_hbm, wd_hbm,
    gate_ref, up_ref, down_ref,
    xv, cv, wgv, wuv, wdv,
    hid, dg, du, mix_a, mix_b,
    stage, perm, xt, xt_b, ct_b,
    nrm_send, nrm_recv,
    xs, xr, zs, zr, sum_a, sum_b,
    a2_0, a2_1, as_0, ar_0, as_1, ar_1,
    b2, bs, br,
    load_sem, nrm_ssem, nrm_rsem, x_ssem, x_rsem, z_ssem, z_rsem, a_ssem, a_rsem, b_ssem, b_rsem,
):
    rows = SLOTS * seq
    dp = lax.axis_index("dp")
    fs = lax.axis_index("fsdp")
    mx = dp // NZ
    mz = dp % NZ

    def at_x(k):
        return (mx + (k + NX)) % NX

    def at_z(k):
        return (mz + (k + NZ)) % NZ

    def x_dev(k):
        return (at_x(k) * NZ + mz, fs)

    def z_dev(k):
        return (mx * NZ + at_z(k), fs)

    def f_dev(k):
        return (dp, (fs + k) % n_f)

    loads = [
        pltpu.make_async_copy(src, dst, load_sem.at[i])
        for i, (src, dst) in enumerate(
            ((x_hbm, xv), (wg_hbm, wgv), (wu_hbm, wuv), (c_hbm, cv), (wd_hbm, wdv))
        )
    ]
    for load in loads:
        load.start()

    barrier = pltpu.get_barrier_semaphore()
    peers = [x_dev(1), x_dev(-1), z_dev(1), z_dev(-1)] + [f_dev(k) for k in range(1, n_f)]
    for peer in peers:
        pl.semaphore_signal(barrier, inc=1, device_id=peer, device_id_type=MESH)

    for buf in (hid, dg, du):
        buf[:, HP - LANE : HP] = jnp.zeros((rows, LANE), BF16)
    for buf in (a2_0, a2_1, b2):
        buf[...] = jnp.zeros_like(buf)
    for load in loads:
        load.wait()

    edges = list(range(0, hidden, 256)) + [hidden]

    def slot_terms(e, carry):
        r = pl.ds(pl.multiple_of(e * seq, seq), seq)
        xe = xv[r, :]
        ce = cv[r, :]
        for lo, hi in zip(edges[:-1], edges[1:]):
            gate_pre = nn(xe, wgv[:, lo:hi])
            up_pre = nn(xe, wuv[:, lo:hi])
            back = nt(ce, wdv[lo:hi, :])
            gelu_value, gelu_slope = gelu_pair(gate_pre)
            hid[r, lo:hi] = (gelu_value * up_pre).astype(BF16)
            dg[r, lo:hi] = (back * up_pre * gelu_slope).astype(BF16)
            du[r, lo:hi] = (back * gelu_value).astype(BF16)
        dge, due, he = dg[r, :], du[r, :], hid[r, :]
        terms = nt(xe, xe) * (nt(dge, dge) + nt(due, due)) + nt(he, he) * nt(ce, ce)
        part = terms[:, 0:LANE]
        for lo in range(LANE, seq, LANE):
            part = part + terms[:, lo : lo + LANE]
        nrm_send[pl.ds(pl.multiple_of(e * 8, 8), 8), :] = part.reshape(seq // 8, 8, LANE).sum(axis=0)
        return carry

    lax.fori_loop(0, SLOTS, slot_terms, 0)

    pl.semaphore_wait(barrier, len(peers))

    def remote(src, dst, ssem, rsem, dev):
        copy = pltpu.make_async_remote_copy(
            src_ref=src, dst_ref=dst, send_sem=ssem, recv_sem=rsem, device_id=dev, device_id_type=MESH
        )
        copy.start()
        return copy

    sends = []
    norm_copies = [
        remote(nrm_send, nrm_recv.at[k - 1], nrm_ssem.at[k - 1], nrm_rsem.at[k - 1], f_dev(k))
        for k in range(1, n_f)
    ]

    def reorder(dst):
        for ox in range(NX):
            for oz in range(NZ):
                src_at = OWN * (NZ * ox + oz)
                dst_at = OWN * (NX * oz + ox)
                dst[dst_at : dst_at + OWN, :] = stage[src_at : src_at + OWN, :]

    turned = xv[...].T
    xt[...] = turned
    stage[...] = turned.astype(F32)
    reorder(perm)
    xt_b[...] = perm[...].astype(BF16)
    stage[...] = cv[...].T.astype(F32)
    reorder(perm)

    for copy in norm_copies:
        copy.wait_recv()
    total = nrm_send[...]
    for k in range(n_f - 1):
        total = total + nrm_recv[k]
    live = live_ref[0]
    for e in range(SLOTS):
        squared = jnp.sum(total[8 * e : 8 * e + 8, :], axis=(0, 1), keepdims=True)
        is_live = jnp.where(e < live, 1.0, 0.0).astype(F32)
        factor = is_live * bound / jnp.maximum(jnp.sqrt(jnp.maximum(squared, 0.0)), bound)
        lo, hi = e * seq, (e + 1) * seq
        ct_b[:, lo:hi] = (perm[:, lo:hi] * factor).astype(BF16)
        mix_b[lo:hi, :] = (du[lo:hi, UP_A:HP].astype(F32) * factor).astype(BF16)
        mix_a[lo:hi, 0:HP] = (dg[lo:hi, :].astype(F32) * factor).astype(BF16)
        mix_a[lo:hi, HP:WA] = (du[lo:hi, 0:UP_A].astype(F32) * factor).astype(BF16)

    def prod_a(chunk, h):
        lo, hi = A_HALF[h]
        r = pl.ds(pl.multiple_of(chunk * XROWS, XROWS), XROWS)
        return nn(xt[r, :], mix_a[:, lo:hi])

    def prod_b(chunk, h):
        lo, hi = B_HALF[h]
        r = pl.ds(pl.multiple_of(chunk * ZROWS, ZROWS), ZROWS)
        if h == 0:
            return jnp.concatenate(
                [nn(xt_b[r, :], mix_b[...]), nn(ct_b[r, :], hid[:, 0 : hi - WU_B])], axis=1
            )
        return nn(ct_b[r, :], hid[:, lo - WU_B : hi - WU_B])

    x_copy = {}

    def x_width(way, step):
        h = (way + step) % 2
        return A_HALF[h][1] - A_HALF[h][0]

    def send_x(step):
        for way in range(2):
            sign = 1 - 2 * way
            h = (way + step) % 2
            dist = 2 if step == 0 else 1
            value = prod_a(at_x(sign * dist), h)
            i = 3 * way + step
            w = x_width(way, step)
            if step == 2:
                x_copy[3 * way].wait_recv()
                value = value + xr[3 * way, :, 0:w].astype(F32)
            xs[i, :, 0:w] = value.astype(BF16)
            x_copy[i] = remote(
                xs.at[i, :, pl.ds(0, w)], xr.at[i, :, pl.ds(0, w)], x_ssem.at[i], x_rsem.at[i], x_dev(sign)
            )

    z_copy = {}

    def send_z(step):
        for way in range(2):
            sign = 1 - 2 * way
            h = (way + step) % 2
            dist = 4 - (step + 1) // 2
            value = prod_b(at_z(sign * dist), h)
            i = 7 * way + step
            if step >= 2:
                z_copy[i - 2].wait_recv()
                value = value + zr[i - 2].astype(F32)
            zs[i] = value.astype(BF16)
            z_copy[i] = remote(zs.at[i], zr.at[i], z_ssem.at[i], z_rsem.at[i], z_dev(sign))

    send_z(0)
    send_x(0)
    send_z(1)
    send_x(1)
    send_z(2)
    send_z(3)
    send_x(2)
    send_z(4)
    send_z(5)
    send_z(6)

    for h in range(2):
        lo, hi = A_HALF[h]
        value = prod_a(mx, h)
        for way in range(2):
            step = 2 if (way + 2) % 2 == h else 1
            i = 3 * way + step
            x_copy[i].wait_recv()
            value = value + xr[i, :, 0 : hi - lo].astype(F32)
        sum_a[:, lo:hi] = value
    a2 = (a2_0, a2_1)
    for oz in range(NZ):
        col = 0
        for h in range(2):
            for t in range(A2_TILES[h]):
                at = oz * A2_ROWS[h] + OWN * t
                a2[h][at : at + OWN, :] = sum_a[OWN * oz : OWN * oz + OWN, col : col + LANE]
                col += LANE

    a_bufs = ((as_0, ar_0), (as_1, ar_1))
    a_copy = {}
    a_slot = {}

    def send_a(step):
        for way in range(2):
            sign = 1 - 2 * way
            h = (way + step) % 2
            dist = 4 - (step + 1) // 2
            n = A2_ROWS[h]
            value = a2[h][pl.ds(pl.multiple_of(at_z(sign * dist) * n, n), n), :]
            i = 7 * way + step
            sbuf, rbuf = a_bufs[h]
            slot = 4 * way + step // 2
            if step >= 2:
                a_copy[i - 2].wait_recv()
                value = value + rbuf[4 * way + (step - 2) // 2].astype(F32)
            sbuf[slot] = value.astype(BF16)
            a_copy[i] = remote(sbuf.at[slot], rbuf.at[slot], a_ssem.at[i], a_rsem.at[i], z_dev(sign))

    send_a(0)
    send_a(1)

    for h in range(2):
        lo, hi = B_HALF[h]
        value = prod_b(mz, h)
        for way in range(2):
            step = 6 if (way + 6) % 2 == h else 5
            i = 7 * way + step
            z_copy[i].wait_recv()
            value = value + zr[i].astype(F32)
        sum_b[:, lo:hi] = value
    for ox in range(NX):
        col = 0
        for h in range(2):
            for t in range(B2_TILES[h]):
                at = ox * B2_ROWS[h] + OWN * t
                b2[h, at : at + OWN, :] = sum_b[OWN * ox : OWN * ox + OWN, col : col + LANE]
                col += LANE

    b_copy = {}

    def send_b(step):
        for way in range(2):
            sign = 1 - 2 * way
            h = (way + step) % 2
            dist = 2 if step == 0 else 1
            n = B2_ROWS[h]
            value = b2[h, pl.ds(pl.multiple_of(at_x(sign * dist) * n, n), n), :]
            i = 3 * way + step
            if step == 2:
                b_copy[3 * way].wait_recv()
                value = value + br[3 * way].astype(F32)
            bs[i] = value.astype(BF16)
            b_copy[i] = remote(bs.at[i], br.at[i], b_ssem.at[i], b_rsem.at[i], x_dev(sign))

    send_b(0)
    send_b(1)
    send_a(2)
    send_a(3)
    send_b(2)
    send_a(4)
    send_a(5)
    send_a(6)

    def put(col, block):
        start, width = col, LANE
        if start < HP:
            ref, at = gate_ref, start
        elif start < 2 * HP:
            ref, at = up_ref, start - HP
        else:
            ref, at = down_ref, start - 2 * HP
        width = min(LANE, hidden - at)
        ref[:, at : at + width] = block[:, 0:width]

    col = WA
    for h in range(2):
        n = B2_ROWS[h]
        value = b2[h, pl.ds(pl.multiple_of(mx * n, n), n), :]
        for way in range(2):
            step = 2 if (way + 2) % 2 == h else 1
            i = 3 * way + step
            b_copy[i].wait_recv()
            value = value + br[i].astype(F32)
        b2[h, 0:n, :] = value
        for t in range(B2_TILES[h]):
            put(col, b2[h, OWN * t : OWN * t + OWN, :])
            col += LANE
    col = 0
    for h in range(2):
        n = A2_ROWS[h]
        value = a2[h][pl.ds(pl.multiple_of(mz * n, n), n), :]
        for way in range(2):
            step = 6 if (way + 6) % 2 == h else 5
            i = 7 * way + step
            a_copy[i].wait_recv()
            value = value + a_bufs[h][1][4 * way + step // 2].astype(F32)
        a2[h][0:n, :] = value
        for t in range(A2_TILES[h]):
            put(col, a2[h][OWN * t : OWN * t + OWN, :])
            col += LANE

    for copies in (norm_copies, x_copy.values(), z_copy.values(), a_copy.values(), b_copy.values()):
        for copy in copies:
            copy.wait_send()


def per_device(
    n_f, inputs, cotangent, gate_weight, up_weight, down_weight, live_counts, noise_gate, noise_up, noise_down
):
    rows = inputs.shape[0]
    seq = rows // SLOTS
    hidden = gate_weight.shape[1]
    bound = 0.1 * math.sqrt(SEQ * D * FF)
    any_spec = pl.BlockSpec(memory_space=pl.ANY)
    vmem = pl.BlockSpec(memory_space=pltpu.VMEM)
    dma = pltpu.SemaphoreType.DMA
    out = jax.ShapeDtypeStruct((OWN, hidden), F32)
    gate, up, down = pl.pallas_call(
        functools.partial(kernel, n_f, seq, hidden, bound),
        out_shape=(out, out, out),
        in_specs=[pl.BlockSpec(memory_space=pltpu.SMEM)] + [any_spec] * 5,
        out_specs=(vmem, vmem, vmem),
        scratch_shapes=[
            pltpu.VMEM((rows, D), BF16),
            pltpu.VMEM((rows, D), BF16),
            pltpu.VMEM((D, hidden), BF16),
            pltpu.VMEM((D, hidden), BF16),
            pltpu.VMEM((hidden, D), BF16),
            pltpu.VMEM((rows, HP), BF16),
            pltpu.VMEM((rows, HP), BF16),
            pltpu.VMEM((rows, HP), BF16),
            pltpu.VMEM((rows, WA), BF16),
            pltpu.VMEM((rows, WU_B), BF16),
            pltpu.VMEM((D, rows), F32),
            pltpu.VMEM((D, rows), F32),
            pltpu.VMEM((D, rows), BF16),
            pltpu.VMEM((D, rows), BF16),
            pltpu.VMEM((D, rows), BF16),
            pltpu.VMEM((8 * SLOTS, LANE), F32),
            pltpu.VMEM((max(n_f - 1, 1), 8 * SLOTS, LANE), F32),
            pltpu.VMEM((6, XROWS, 768), BF16),
            pltpu.VMEM((6, XROWS, 768), BF16),
            pltpu.VMEM((14, ZROWS, 640), BF16),
            pltpu.VMEM((14, ZROWS, 640), BF16),
            pltpu.VMEM((XROWS, WA), F32),
            pltpu.VMEM((ZROWS, WB), F32),
            pltpu.VMEM((NZ * A2_ROWS[0], LANE), F32),
            pltpu.VMEM((NZ * A2_ROWS[1], LANE), F32),
            pltpu.VMEM((8, A2_ROWS[0], LANE), BF16),
            pltpu.VMEM((8, A2_ROWS[0], LANE), BF16),
            pltpu.VMEM((8, A2_ROWS[1], LANE), BF16),
            pltpu.VMEM((8, A2_ROWS[1], LANE), BF16),
            pltpu.VMEM((2, NX * B2_ROWS[0], LANE), F32),
            pltpu.VMEM((6, B2_ROWS[0], LANE), BF16),
            pltpu.VMEM((6, B2_ROWS[0], LANE), BF16),
            dma((5,)),
            dma((max(n_f - 1, 1),)),
            dma((max(n_f - 1, 1),)),
            dma((6,)),
            dma((6,)),
            dma((14,)),
            dma((14,)),
            dma((14,)),
            dma((14,)),
            dma((6,)),
            dma((6,)),
        ],
        compiler_params=pltpu.CompilerParams(
            collective_id=0, has_side_effects=True, vmem_limit_bytes=60 * 1024 * 1024
        ),
    )(live_counts, inputs, cotangent, gate_weight, up_weight, down_weight)
    return gate + noise_gate, up + noise_up, down.T + noise_down


def solution(mesh):
    in_specs = (
        P("dp", None),
        P("dp", None),
        P(None, "fsdp"),
        P(None, "fsdp"),
        P("fsdp", None),
        P("dp"),
        P("dp", "fsdp"),
        P("dp", "fsdp"),
        P("fsdp", "dp"),
    )
    out_specs = (P("dp", "fsdp"), P("dp", "fsdp"), P("fsdp", "dp"))
    return jax.shard_map(
        functools.partial(per_device, mesh.shape["fsdp"]),
        mesh=mesh, in_specs=in_specs, out_specs=out_specs, check_vma=False,
    )
```

time: 361 us -> 84.8 us (0.23)
  waiting for transfers between devices: 257 us -> 0 us
  Pallas kernels: 0 us -> 70.5 us
  matrix products: 35.4 us -> 0 us
  between operations: 23.6 us -> 1.31 us
  blocking collectives: 15.4 us -> 0 us
  local copies, waits for them, and re-layouts: 16.5 us -> 6.68 us
  other arithmetic: 12.9 us -> 4.76 us
    unnamed x2 -> x0, waiting for transfers between devices: 257 us -> none
    pallas_call x0 -> x1, Pallas kernels: none -> 70.5 us  [per_device(): pl.pallas_call(functools.partial(kernel, n_f, seq, hidden, bound), out_sh...]
    dot_general x20 -> x0, matrix products: 35.4 us -> none  [the longest x11 23.9 us: outer_rows(): lax.dot_general(left_side, right_side, (((0,), (0,)), ((), ())), preferre...]
    psum x1 -> x0, blocking collectives: 15.4 us -> none  [per_device(): squared = lax.psum(partial_value, 'fsdp')]
    dynamic_update_slice x4 -> x0, local copies, waits for them, and re-layouts: 6.59 us -> none  [the longest x2 6.37 us: per_device(): lax.dynamic_update_index_in_dim(run_mix_buf, mixed, slot_index, 0)]
    concatenate x1 -> x0, other arithmetic: 4.72 us -> none  [per_device(): jnp.concatenate([gate_block, down_block], axis=1)]
    unnamed x47 -> x10, local copies, waits for them, and re-layouts: 9.89 us -> 6.68 us
  transfers between devices with their start and end apart: 1 -> 0, of which waited for: 1 -> 0; matrix products, arithmetic and copies ran while one was open for 0% -> 0% of each run, Pallas kernels for 0% -> 0%
where the time goes in v1:
time: 84.8 us; the launch traced here: 83.3 us
  Pallas kernels  70.5 us (83%)
  local copies, waits for them, and re-layouts  6.68 us (8%)
  other arithmetic  4.76 us (6%)
  between operations  1.31 us (2%)
    pallas_call x1, Pallas kernels, per_device(): pl.pallas_call(functools.partial(kernel, n_f, seq, hidden, bound), out_sh...  70.5 us
    unnamed x10, local copies, waits for them, and re-layouts  6.68 us
    add x3, other arithmetic, per_device(): return (gate + noise_gate, up + noise_up, down.T + noise_down)  4.76 us

profile of v1, /device:TPU:2, one launch (start us, length us, event | category | flops | bytes accessed | tf_op | source)
XLA Modules:
  0.0 83.3 jit_solution(3527995464945177416)
XLA Ops:
  1.3 0.0 copy-start
  1.3 4.2 %copy.12.wg_hbm = bf16[1152,864]{1,0:T(8,128)(2,1)} copy(bf16[1152,864]{0,1:T(8,128)(2,1)} %param.11) | data formatting | bytes 3981312 | tf_op args[2]
  5.5 0.0 copy-done
  5.5 2.4 %copy.13.wu_hbm = bf16[1152,864]{1,0:T(8,128)(2,1)} copy(bf16[1152,864]{0,1:T(8,128)(2,1)S(1)} %copy-done) | data formatting | bytes 3981312 | tf_op args[3]
  8.0 0.0 copy-start.1
  8.0 0.0 copy-start.2
  8.0 0.0 copy-start.3
  8.0 70.5 %shard_map.112 = (f32[36,864]{1,0:T(8,128)}, f32[36,864]{1,0:T(8,128)}, f32[36,864]{1,0:T(8,128)}) custom-call(s32[1]{0:T(128)S(6)} %copy.14.live_ref, bf16[768,1152]{1,0:T(8,128)(2,1)} %x_hbm.1, bf16[768,1152]{1,0:T(8,128)(2,1)} %c_hbm.1, bf16[1152,864]{1,0:T(8,128)(2,1)} %copy.12.wg_hbm, bf16[1152,864]{1,0:T(8,128)(2,1)} %copy.13.wu_hbm, ...), custom_call_target="tpu_custom_call" | custom-call | tf_op jit(solution)/shard_map/pallas_call | solution.py:390
  78.5 0.0 copy-done.1
  78.5 1.6 %add.9 = f32[36,864]{1,0:T(8,128)} add(f32[36,864]{1,0:T(8,128)} %get-tuple-element.6, f32[36,864]{1,0:T(8,128)S(1)} %copy-done.1) | non-fusion elementwise | flops 31104 | bytes 373248 | tf_op jit(solution)/shard_map/add | solution.py:444
  80.1 0.0 copy-done.2
  80.1 1.6 %add.10 = f32[36,864]{1,0:T(8,128)} add(f32[36,864]{1,0:T(8,128)} %get-tuple-element.7, f32[36,864]{1,0:T(8,128)S(1)} %copy-done.2) | non-fusion elementwise | flops 31104 | bytes 373248 | tf_op jit(solution)/shard_map/add | solution.py:444
  81.7 0.0 copy-done.3
  81.7 1.6 %bitcast_add_fusion = f32[864,36]{0,1:T(8,128)} fusion(f32[864,36]{0,1:T(8,128)S(1)} %copy-done.3, f32[36,864]{1,0:T(8,128)} %get-tuple-element.8), kind=kLoop, calls=%fused_computation | loop fusion | flops 31104 | bytes 373248 | tf_op jit(solution)/shard_map/add | solution.py:444
Async XLA Ops:
  1.3 4.2 %copy-start = (bf16[1152,864]{0,1:T(8,128)(2,1)S(1)}, bf16[1152,864]{0,1:T(8,128)(2,1)}, u32[]{:S(2)}) copy-start(bf16[1152,864]{0,1:T(8,128)(2,1)} %param.12) | copy-start | bytes 5971972
  8.0 70.5 %copy-start.1 = (f32[36,864]{1,0:T(8,128)S(1)}, f32[36,864]{1,0:T(8,128)}, u32[]{:S(2)}) copy-start(f32[36,864]{1,0:T(8,128)} %param.15) | copy-start | bytes 373252
  8.0 72.1 %copy-start.2 = (f32[36,864]{1,0:T(8,128)S(1)}, f32[36,864]{1,0:T(8,128)}, u32[]{:S(2)}) copy-start(f32[36,864]{1,0:T(8,128)} %param.16) | copy-start | bytes 373252
  8.0 73.7 %copy-start.3 = (f32[864,36]{0,1:T(8,128)S(1)}, f32[864,36]{0,1:T(8,128)}, u32[]{:S(2)}) copy-start(f32[864,36]{0,1:T(8,128)} %param.17) | copy-start | bytes 373252

commit v2 on v0

v2 whole, which is shorter than its diff:
```python
import functools
import math

import jax
import jax.numpy as jnp
from jax import lax
from jax.experimental import pallas as pl
from jax.experimental.pallas import tpu as pltpu
from jax.sharding import PartitionSpec as P

D = 1152
FF = 6912
SEQ = 256
SLOTS = 3
NX = 4
NZ = 8
OWN = D // (NX * NZ)
XROWS = D // NX
ZROWS = D // NZ
LANE = 128
F32 = jnp.float32
BF16 = jnp.bfloat16
MESH = pl.DeviceIdType.MESH

gelu_scale = 0.7978845608028654
gelu_cube = 0.044715

HP = 896
GROUPS = (
    ("z", ((("up", 512, 896),), (("down", 0, 256),)), "direct"),
    ("x", ((("gate", 0, 512),), (("gate", 512, 896), ("up", 0, 128),)), "chain"),
    ("z", ((("down", 256, 512),), (("down", 512, 896),)), "direct"),
    ("x", ((("up", 128, 384),), (("up", 384, 512),)), "tree"),
)
ORDER = (
    (2, 1, 0), (1, 1, 0), (2, 1, 1), (0, 1, 0), (0, 1, 1), (1, 1, 1), (2, 1, 2), (2, 1, 3),
    (0, 1, 2), (1, 1, 2), (0, 1, 3), (2, 1, 4), (2, 1, 5), (3, 1, 0), (0, 1, 4), (3, 1, 1),
    (0, 1, 5), (1, 0, 0), (2, 1, 6), (1, 2, 0), (3, 1, 2), (1, 2, 1), (0, 1, 6), (2, 0, 0),
    (2, 2, 0), (1, 2, 2), (1, 2, 3), (3, 0, 0), (3, 2, 0), (3, 2, 1), (0, 0, 0), (0, 2, 0),
    (1, 2, 4), (1, 2, 5), (2, 3, 0), (3, 2, 2), (1, 2, 6), (0, 3, 0), (3, 3, 0), (1, 3, 0),
)
RING = {"x": NX, "z": NZ}


def pad16(n):
    return (n + 15) // 16 * 16


def gelu_pair(values):
    square = values * values
    tangent = jnp.tanh(values * (gelu_scale + (gelu_scale * gelu_cube) * square))
    half_sum = 0.5 + 0.5 * tangent
    gelu_value = values * half_sum
    gelu_slope = half_sum + (0.5 * values) * (1.0 - tangent * tangent) * (
        gelu_scale + (3.0 * gelu_scale * gelu_cube) * square
    )
    return gelu_value, gelu_slope


def nt(a, b):
    return lax.dot_general(a, b, (((1,), (1,)), ((), ())), preferred_element_type=F32)


def nn(a, b):
    return lax.dot_general(a, b, (((1,), (0,)), ((), ())), preferred_element_type=F32)


def width_of(half):
    return sum(hi - lo for _, lo, hi in half)


def chain(axis):
    last, far = (3, 2) if axis == "x" else (7, 4)
    sends = []
    for step in range(last):
        for way in range(2):
            sign = 1 - 2 * way
            halves = ((way + step) % 2,)
            owner = sign * (far - (step + 1) // 2)
            sends.append((step, way, halves, owner, sign, (len(sends) - 4,) if step >= 2 else ()))
    return sends


def direct(axis):
    far = RING[axis] // 2
    sends = []
    for dist in range(far, 0, -1):
        for way in range(2):
            at = dist * (1 - 2 * way)
            sends.append((0, way, (way,) if dist == far else (0, 1), at, at, ()))
    return sends


def tree(axis):
    sends = []
    for way in range(2):
        sign = 1 - 2 * way
        sends.append((0, way, (way,), 4 * sign, 2 * sign, ()))
    for way in range(2):
        sign = 1 - 2 * way
        sends.append((0, way, (0, 1), 3 * sign, sign, ()))
    for way in range(2):
        sign = 1 - 2 * way
        sends.append((1, way, (0, 1), sign, sign, ()))
    for way in range(2):
        sign = 1 - 2 * way
        sends.append((2, way, (0, 1), 2 * sign, 2 * sign, (way, 2 + way)))
    return sends


SECOND = {"chain": chain, "direct": direct, "tree": tree}


def packed_rows(g):
    return [pad16(OWN * width_of(half) // LANE) for half in GROUPS[g][1]]


def plan():
    sends = {}
    for g, (axis, _, mode) in enumerate(GROUPS):
        other = "z" if axis == "x" else "x"
        sends[g, 1] = (axis, chain(axis))
        sends[g, 2] = (other, SECOND[mode](other))
    return sends


def scratch_plan():
    shapes = {}
    for g, (axis, halves, _) in enumerate(GROUPS):
        rows = XROWS if axis == "x" else ZROWS
        other = NZ if axis == "x" else NX
        first = RING[axis] - 1
        for h, half in enumerate(halves):
            width = width_of(half)
            shapes[g, h, "s1"] = ((first, rows, width), BF16)
            shapes[g, h, "r1"] = ((first, rows, width), BF16)
            shapes[g, h, "sum"] = ((rows, width), F32)
        packed = packed_rows(g)
        shapes[g, "pack"] = ((other * sum(packed), LANE), F32)
        total = sum(packed[h] for send in plan()[g, 2][1] for h in send[2])
        shapes[g, "s2"] = ((total, LANE), BF16)
        shapes[g, "r2"] = ((total, LANE), BF16)
    return shapes


def total_sends():
    return sum(len(sends) for _, sends in plan().values())


def kernel(
    n_f, seq, hidden, bound,
    live_ref, x_hbm, c_hbm, wg_hbm, wu_hbm, wd_hbm,
    gate_ref, up_ref, down_ref,
    xv, cv, wgv, wuv, wrem, wdv,
    hid, dg, du,
    stage, perm, xt, xt_z, ct_z,
    nrm_send, nrm_recv,
    fin, load_sem, nrm_ssem, nrm_rsem, ssem, rsem,
    *group_refs,
):
    rows = SLOTS * seq
    dp = lax.axis_index("dp")
    fs = lax.axis_index("fsdp")
    mine = {"x": dp // NZ, "z": dp % NZ}
    buf = dict(zip(scratch_plan(), group_refs))

    def at(axis, k):
        return (mine[axis] + (k + RING[axis])) % RING[axis]

    def neighbour(axis, k):
        if axis == "x":
            return (at("x", k) * NZ + mine["z"], fs)
        return (mine["x"] * NZ + at("z", k), fs)

    def f_dev(k):
        return (dp, (fs + k) % n_f)

    full = hidden // 256 * 256
    rest = hidden - full
    pairs = [(x_hbm, xv)]
    for lo in range(0, full, 256):
        r = pl.ds(lo, 256)
        pairs += [(wg_hbm.at[r, :], wgv.at[r, :]), (wu_hbm.at[r, :], wuv.at[r, :])]
        if lo == 0:
            pairs.append((c_hbm, cv))
        pairs.append((wd_hbm.at[r, :], wdv.at[r, :]))
    r = pl.ds(full, rest)
    pairs.append((wg_hbm.at[r, :], wrem.at[pl.ds(0, rest), :]))
    pairs.append((wu_hbm.at[r, :], wrem.at[pl.ds(LANE, rest), :]))
    pairs.append((wd_hbm.at[r, :], wdv.at[r, :]))
    loads = [pltpu.make_async_copy(src, dst, load_sem.at[i]) for i, (src, dst) in enumerate(pairs)]
    for load in loads:
        load.start()

    barrier = pltpu.get_barrier_semaphore()
    reached = sorted({(axis, send[4] % RING[axis]) for axis, sends in plan().values() for send in sends})
    peers = [neighbour(axis, k) for axis, k in reached]
    peers += [f_dev(k) for k in range(1, n_f)]
    for peer in peers:
        pl.semaphore_signal(barrier, inc=1, device_id=peer, device_id_type=MESH)

    for ref in (hid, dg, du):
        ref[:, HP - LANE : HP] = jnp.zeros((rows, LANE), BF16)
    wrem[rest:LANE, :] = jnp.zeros((LANE - rest, D), BF16)
    wrem[LANE + rest : 2 * LANE, :] = jnp.zeros((LANE - rest, D), BF16)
    for key, ref in buf.items():
        if key[-1] == "pack":
            ref[...] = jnp.zeros_like(ref)

    blocks = [(lo, lo + 256) for lo in range(0, full, 256)] + [(full, hidden)]
    step_rows = rows // 2

    def products(lo, hi, r):
        if lo < full:
            return nt(xv[r, :], wgv[lo:hi, :]), nt(xv[r, :], wuv[lo:hi, :]), nt(cv[r, :], wdv[lo:hi, :])
        both = nt(xv[r, :], wrem[...])
        return both[:, 0:rest], both[:, LANE : LANE + rest], nt(cv[r, :], wdv[lo:hi, :])

    def terms(lo, hi, r, gate_pre, up_pre, back):
        gelu_value, gelu_slope = gelu_pair(gate_pre)
        hid[r, lo:hi] = (gelu_value * up_pre).astype(BF16)
        dg[r, lo:hi] = (back * up_pre * gelu_slope).astype(BF16)
        du[r, lo:hi] = (back * gelu_value).astype(BF16)

    row_blocks = [slice(lo, lo + step_rows) for lo in range(0, rows, step_rows)]
    taken = 0
    before = None
    for i, (lo, hi) in enumerate(blocks):
        count = 5 if i == 0 else 3
        for load in loads[taken : taken + count]:
            load.wait()
        taken += count
        now = []
        for j, r in enumerate(row_blocks):
            now.append(products(lo, hi, r))
            if before is not None:
                terms(*blocks[i - 1], r, *before[j])
        before = now
    for load in loads[taken:]:
        load.wait()

    slot_rows = [slice(e * seq, (e + 1) * seq) for e in range(SLOTS)]
    gram_x = [nt(xv[r, :], xv[r, :]) for r in slot_rows]
    gram_c = [nt(cv[r, :], cv[r, :]) for r in slot_rows]
    for j, r in enumerate(row_blocks):
        terms(*blocks[-1], r, *before[j])
    for e, r in enumerate(slot_rows):
        dge, due, he = dg[r, :], du[r, :], hid[r, :]
        prod = gram_x[e] * (nt(dge, dge) + nt(due, due)) + nt(he, he) * gram_c[e]
        part = prod[:, 0:LANE]
        for lo in range(LANE, seq, LANE):
            part = part + prod[:, lo : lo + LANE]
        nrm_send[8 * e : 8 * e + 8, :] = part.reshape(seq // 8, 8, LANE).sum(axis=0)

    pl.semaphore_wait(barrier, len(peers))

    sent = []

    def remote(src, dst, send_sem, recv_sem, dev):
        copy = pltpu.make_async_remote_copy(
            src_ref=src, dst_ref=dst, send_sem=send_sem, recv_sem=recv_sem, device_id=dev, device_id_type=MESH
        )
        copy.start()
        sent.append(copy)
        return copy

    norm_copies = [
        remote(nrm_send, nrm_recv.at[k - 1], nrm_ssem.at[k - 1], nrm_rsem.at[k - 1], f_dev(k))
        for k in range(1, n_f)
    ]

    def reorder(dst):
        for ox in range(NX):
            for oz in range(NZ):
                src_at = OWN * (NZ * ox + oz)
                dst_at = OWN * (NX * oz + ox)
                dst[dst_at : dst_at + OWN, :] = stage[src_at : src_at + OWN, :]

    turned = xv[...].T
    xt[...] = turned
    stage[...] = turned.astype(F32)
    reorder(perm)
    xt_z[...] = perm[...].astype(BF16)
    stage[...] = cv[...].T.astype(F32)
    reorder(perm)

    for copy in norm_copies:
        copy.wait_recv()
    total = nrm_send[...]
    for k in range(n_f - 1):
        total = total + nrm_recv[k]
    live = live_ref[0]
    factors = []
    for e in range(SLOTS):
        squared = jnp.sum(total[8 * e : 8 * e + 8, :], axis=(0, 1), keepdims=True)
        is_live = jnp.where(e < live, 1.0, 0.0).astype(F32)
        factors.append(is_live * bound / jnp.maximum(jnp.sqrt(jnp.maximum(squared, 0.0)), bound))

    matrix = {"gate": dg, "up": du, "down": hid}
    scaled = set()

    def right_side(src, lo, hi):
        if src != "down" and (src, lo) not in scaled:
            scaled.add((src, lo))
            for e in range(SLOTS):
                r = slice(e * seq, (e + 1) * seq)
                matrix[src][r, lo:hi] = (matrix[src][r, lo:hi].astype(F32) * factors[e]).astype(BF16)
        return matrix[src][:, lo:hi]

    def left_side(axis, src, k):
        n = XROWS if axis == "x" else ZROWS
        r = pl.ds(pl.multiple_of(at(axis, k) * n, n), n)
        if src != "down":
            return xt[r, :] if axis == "x" else xt_z[r, :]
        if k not in scaled:
            scaled.add(k)
            for e in range(SLOTS):
                c = slice(e * seq, (e + 1) * seq)
                ct_z[r, c] = (perm[r, c] * factors[e]).astype(BF16)
        return ct_z[r, :]

    def product(g, h, k):
        axis, halves, _ = GROUPS[g]
        parts = []
        for src, lo, hi in halves[h]:
            right = right_side(src, lo, hi)
            parts.append(nn(left_side(axis, src, k), right))
        return parts[0] if len(parts) == 1 else jnp.concatenate(parts, axis=1)

    routes = plan()
    copies = {}
    spot = {}
    numbers = {}
    for (g, phase), (ring, sends) in routes.items():
        used = [0, 0]
        row = 0
        packed = packed_rows(g)
        for i, (step, way, halves, owner, target, adds) in enumerate(sends):
            numbers[g, phase, i] = len(numbers)
            if phase == 1:
                spot[g, phase, i] = (used[halves[0]],)
                used[halves[0]] += 1
            else:
                n = sum(packed[h] for h in halves)
                spot[g, phase, i] = (row, n)
                row += n

    def received(g, phase, i, h):
        if phase == 1:
            return buf[g, h, "r1"][spot[g, phase, i][0]].astype(F32)
        row, _ = spot[g, phase, i]
        packed = packed_rows(g)
        for half in routes[g, phase][1][i][2]:
            if half == h:
                return buf[g, "r2"][row : row + packed[h], :].astype(F32)
            row += packed[half]

    def send(g, phase, step):
        ring, sends = routes[g, phase]
        packed = packed_rows(g)
        for i, (at_step, way, halves, owner, target, adds) in enumerate(sends):
            if at_step != step:
                continue
            values = []
            for h in halves:
                if phase == 1:
                    value = product(g, h, owner)
                else:
                    n = sum(packed)
                    first = pl.multiple_of(at(ring, owner) * n, n) + (packed[0] if h else 0)
                    value = buf[g, "pack"][pl.ds(pl.multiple_of(first, 16), packed[h]), :]
                values.append(value)
            for j in adds:
                copies[g, phase, j].wait_recv()
                for k, h in enumerate(halves):
                    if h in sends[j][2]:
                        values[k] = values[k] + received(g, phase, j, h)
            if phase == 1:
                h, slot = halves[0], spot[g, phase, i][0]
                src, dst = buf[g, h, "s1"].at[slot], buf[g, h, "r1"].at[slot]
                src[...] = values[0].astype(BF16)
            else:
                row, n = spot[g, phase, i]
                src, dst = buf[g, "s2"].at[pl.ds(row, n), :], buf[g, "r2"].at[pl.ds(row, n), :]
                for k, h in enumerate(halves):
                    buf[g, "s2"][row : row + packed[h], :] = values[k].astype(BF16)
                    row += packed[h]
            number = numbers[g, phase, i]
            copies[g, phase, i] = remote(src, dst, ssem.at[number], rsem.at[number], neighbour(ring, target))

    def arrived(g, phase, h, value):
        for i, (_, _, halves, owner, target, _) in enumerate(routes[g, phase][1]):
            if owner == target and h in halves:
                if (g, phase, i) not in waited:
                    waited.add((g, phase, i))
                    copies[g, phase, i].wait_recv()
                value = value + received(g, phase, i, h)
        return value

    waited = set()

    def close_first(g):
        axis, halves, _ = GROUPS[g]
        packed = packed_rows(g)
        for h, half in enumerate(halves):
            full_sum, pack = buf[g, h, "sum"], buf[g, "pack"]
            full_sum[...] = arrived(g, 1, h, product(g, h, 0))
            for o in range(NZ if axis == "x" else NX):
                for t in range(width_of(half) // LANE):
                    to = o * sum(packed) + (packed[0] if h else 0) + OWN * t
                    pack[to : to + OWN, :] = full_sum[OWN * o : OWN * o + OWN, LANE * t : LANE * t + LANE]

    out = {"gate": gate_ref, "up": up_ref, "down": down_ref}

    def close_second(g):
        axis, halves, _ = GROUPS[g]
        packed = packed_rows(g)
        n = sum(packed)
        pack = buf[g, "pack"]
        base = mine["z" if axis == "x" else "x"] * n
        for h, half in enumerate(halves):
            row = packed[0] if h else 0
            own = pack[pl.ds(pl.multiple_of(pl.multiple_of(base, n) + row, 16), packed[h]), :]
            buf_sum = fin.at[pl.ds(row, packed[h]), :]
            buf_sum[...] = arrived(g, 2, h, own)
            for src, lo, hi in half:
                for start in range(lo, hi, LANE):
                    width = min(LANE, hidden - start)
                    out[src][:, start : start + width] = fin[row : row + OWN, 0:width]
                    row += OWN

    for g, phase, step in ORDER:
        if phase == 0:
            close_first(g)
        elif phase == 3:
            close_second(g)
        else:
            send(g, phase, step)

    for copy in sent:
        copy.wait_send()


def add_noise(gate_ref, up_ref, down_ref, ng_ref, nu_ref, nd_ref, gate_out, up_out, down_out):
    gate_out[...] = gate_ref[...] + ng_ref[...]
    up_out[...] = up_ref[...] + nu_ref[...]
    down_out[...] = down_ref[...] + nd_ref[...]


def per_device(
    n_f, inputs, cotangent, gate_weight, up_weight, down_weight, live_counts, noise_gate, noise_up, noise_down
):
    rows = inputs.shape[0]
    seq = rows // SLOTS
    hidden = gate_weight.shape[1]
    full = hidden // 256 * 256
    bound = 0.1 * math.sqrt(SEQ * D * FF)
    any_spec = pl.BlockSpec(memory_space=pl.ANY)
    vmem = pl.BlockSpec(memory_space=pltpu.VMEM)
    dma = pltpu.SemaphoreType.DMA
    out = jax.ShapeDtypeStruct((OWN, hidden), F32)
    gate, up, down = pl.pallas_call(
        functools.partial(kernel, n_f, seq, hidden, bound),
        out_shape=(out, out, out),
        in_specs=[pl.BlockSpec(memory_space=pltpu.SMEM)] + [any_spec] * 5,
        out_specs=(vmem, vmem, vmem),
        scratch_shapes=[
            pltpu.VMEM((rows, D), BF16),
            pltpu.VMEM((rows, D), BF16),
            pltpu.VMEM((full, D), BF16),
            pltpu.VMEM((full, D), BF16),
            pltpu.VMEM((2 * LANE, D), BF16),
            pltpu.VMEM((hidden, D), BF16),
            pltpu.VMEM((rows, HP), BF16),
            pltpu.VMEM((rows, HP), BF16),
            pltpu.VMEM((rows, HP), BF16),
            pltpu.VMEM((D, rows), F32),
            pltpu.VMEM((D, rows), F32),
            pltpu.VMEM((D, rows), BF16),
            pltpu.VMEM((D, rows), BF16),
            pltpu.VMEM((D, rows), BF16),
            pltpu.VMEM((8 * SLOTS, LANE), F32),
            pltpu.VMEM((max(n_f - 1, 1), 8 * SLOTS, LANE), F32),
            pltpu.VMEM((max(sum(packed_rows(g)) for g in range(len(GROUPS))), LANE), F32),
            dma((2 + 3 * (full // 256) + 3,)),
            dma((max(n_f - 1, 1),)),
            dma((max(n_f - 1, 1),)),
            dma((total_sends(),)),
            dma((total_sends(),)),
        ]
        + [pltpu.VMEM(shape, dtype) for shape, dtype in scratch_plan().values()],
        compiler_params=pltpu.CompilerParams(
            collective_id=0, has_side_effects=True, vmem_limit_bytes=60 * 1024 * 1024
        ),
    )(live_counts, inputs, cotangent, gate_weight.T, up_weight.T, down_weight)
    gate, up, down = pl.pallas_call(
        add_noise,
        out_shape=(out, out, out),
        in_specs=[vmem] * 6,
        out_specs=(vmem, vmem, vmem),
    )(gate, up, down, noise_gate, noise_up, noise_down.T)
    return gate, up, down.T


def solution(mesh):
    in_specs = (
        P("dp", None),
        P("dp", None),
        P(None, "fsdp"),
        P(None, "fsdp"),
        P("fsdp", None),
        P("dp"),
        P("dp", "fsdp"),
        P("dp", "fsdp"),
        P("fsdp", "dp"),
    )
    out_specs = (P("dp", "fsdp"), P("dp", "fsdp"), P("fsdp", "dp"))
    return jax.shard_map(
        functools.partial(per_device, mesh.shape["fsdp"]),
        mesh=mesh, in_specs=in_specs, out_specs=out_specs, check_vma=False,
    )
```

time: 361 us -> 69.8 us (0.19)
  waiting for transfers between devices: 257 us -> 0 us
  Pallas kernels: 0 us -> 68.4 us
  matrix products: 35.4 us -> 0 us
  between operations: 23.6 us -> 1.29 us
  local copies, waits for them, and re-layouts: 16.5 us -> 0 us
  blocking collectives: 15.4 us -> 0 us
  other arithmetic: 12.9 us -> 0 us
    unnamed x2 -> x0, waiting for transfers between devices: 257 us -> none
    pallas_call x0 -> x2, Pallas kernels: none -> 68.4 us  [the longest x1 66.4 us: per_device(): pl.pallas_call(functools.partial(kernel, n_f, seq, hidden, bound), out_sh...]
    dot_general x20 -> x0, matrix products: 35.4 us -> none  [the longest x11 23.9 us: outer_rows(): lax.dot_general(left_side, right_side, (((0,), (0,)), ((), ())), preferre...]
    psum x1 -> x0, blocking collectives: 15.4 us -> none  [per_device(): squared = lax.psum(partial_value, 'fsdp')]
    unnamed x47 -> x0, local copies, waits for them, and re-layouts: 9.89 us -> none
    dynamic_update_slice x4 -> x0, local copies, waits for them, and re-layouts: 6.59 us -> none  [the longest x2 6.37 us: per_device(): lax.dynamic_update_index_in_dim(run_mix_buf, mixed, slot_index, 0)]
    concatenate x1 -> x0, other arithmetic: 4.72 us -> none  [per_device(): jnp.concatenate([gate_block, down_block], axis=1)]
    add x2 -> x0, other arithmetic: 4.17 us -> none  [the longest x1 2.82 us: per_device(): grad_up = my_share[:, hidden_local:2 * hidden_local] + noise_up]
  transfers between devices with their start and end apart: 1 -> 0, of which waited for: 1 -> 0; matrix products, arithmetic and copies ran while one was open for 0% -> 0% of each run, Pallas kernels for 0% -> 0%
where the time goes in v2:
time: 69.8 us; the launch traced here: 69.7 us
  Pallas kernels  68.4 us (98%)
  between operations  1.29 us (2%)
    pallas_call x1, Pallas kernels, per_device(): pl.pallas_call(functools.partial(kernel, n_f, seq, hidden, bound), out_sh...  66.4 us
    pallas_call x1, Pallas kernels, per_device(): pl.pallas_call(add_noise, out_shape=(out, out, out), in_specs=[vmem] * 6,...  2.01 us

profile of v2, /device:TPU:2, one launch (start us, length us, event | category | flops | bytes accessed | tf_op | source)
XLA Modules:
  0.0 69.7 jit_solution(5701664900422432639)
XLA Ops:
  1.3 66.4 %shard_map.112 = (f32[36,864]{1,0:T(8,128)}, f32[36,864]{1,0:T(8,128)}, f32[36,864]{1,0:T(8,128)}) custom-call(s32[1]{0:T(128)S(6)} %copy.12.live_ref, bf16[768,1152]{1,0:T(8,128)(2,1)} %x_hbm.1, bf16[768,1152]{1,0:T(8,128)(2,1)} %c_hbm.1, bf16[864,1152]{1,0:T(8,128)(2,1)} %bitcast.4, bf16[864,1152]{1,0:T(8,128)(2,1)} %bitcast.5, bf16[864,1152]{1,0:T(8,128)(2,1)} %wd_hbm.1), custom_call_target="tpu_custom_call" | custom-call | tf_op jit(solution)/shard_map/pallas_call | solution.py:462
  67.7 2.0 %shard_map.113 = (f32[36,864]{1,0:T(8,128)}, f32[36,864]{1,0:T(8,128)}, f32[36,864]{1,0:T(8,128)}) custom-call(f32[36,864]{1,0:T(8,128)} %get-tuple-element.9.gate_ref, f32[36,864]{1,0:T(8,128)} %get-tuple-element.10.up_ref, f32[36,864]{1,0:T(8,128)} %get-tuple-element.11.down_ref, f32[36,864]{1,0:T(8,128)} %ng_ref.1, f32[36,864]{1,0:T(8,128)} %nu_ref.1, ...), custom_call_target="tpu_custom_call" | custom-call | tf_op jit(solution)/shard_map/pallas_call | solution.py:496

commit v3 on v2

--- a/solution.py
+++ b/solution.py
@@ -152,7 +152,7 @@
     live_ref, x_hbm, c_hbm, wg_hbm, wu_hbm, wd_hbm,
     gate_ref, up_ref, down_ref,
     xv, cv, wgv, wuv, wrem, wdv,
-    hid, dg, du,
+    hid, dg, du, gram_x,
     stage, perm, xt, xt_z, ct_z,
     nrm_send, nrm_recv,
     fin, load_sem, nrm_ssem, nrm_rsem, ssem, rsem,
@@ -199,6 +199,54 @@
     for peer in peers:
         pl.semaphore_signal(barrier, inc=1, device_id=peer, device_id_type=MESH)
 
+    blocks = [(lo, lo + 256) for lo in range(0, full, 256)] + [(full, hidden)]
+    step_rows = rows // 2
+
+    def products(lo, hi, r):
+        if lo < full:
+            yield nt(xv[r, :], wgv[lo:hi, :])
+            yield nt(xv[r, :], wuv[lo:hi, :])
+        else:
+            both = nt(xv[r, :], wrem[...])
+            yield both[:, 0:rest]
+            yield both[:, LANE : LANE + rest]
+        yield nt(cv[r, :], wdv[lo:hi, :])
+
+    def terms(lo, hi, r, gate_pre, up_pre, back):
+        gelu_value, gelu_slope = gelu_pair(gate_pre)
+        hid[r, lo:hi] = (gelu_value * up_pre).astype(BF16)
+        dg[r, lo:hi] = (back * up_pre * gelu_slope).astype(BF16)
+        du[r, lo:hi] = (back * gelu_value).astype(BF16)
+
+    def reorder(dst):
+        for ox in range(NX):
+            for oz in range(NZ):
+                src_at = OWN * (NZ * ox + oz)
+                dst_at = OWN * (NX * oz + ox)
+                dst[dst_at : dst_at + OWN, :] = stage[src_at : src_at + OWN, :]
+
+    def turn(k):
+        if k == 0:
+            turned = xv[...].T
+            xt[...] = turned
+            stage[...] = turned.astype(F32)
+        elif k == 1:
+            reorder(perm)
+        elif k == 2:
+            xt_z[...] = perm[...].astype(BF16)
+        elif k == 3:
+            stage[...] = cv[...].T.astype(F32)
+        elif k == 4:
+            reorder(perm)
+
+    row_blocks = [slice(lo, lo + step_rows) for lo in range(0, rows, step_rows)]
+    taken = 0
+    before = None
+    loads[0].wait()
+    taken = 1
+    slot_rows = [slice(e * seq, (e + 1) * seq) for e in range(SLOTS)]
+    for e, r in enumerate(slot_rows):
+        gram_x[e] = nt(xv[r, :], xv[r, :])
     for ref in (hid, dg, du):
         ref[:, HP - LANE : HP] = jnp.zeros((rows, LANE), BF16)
     wrem[rest:LANE, :] = jnp.zeros((LANE - rest, D), BF16)
@@ -206,41 +254,28 @@
     for key, ref in buf.items():
         if key[-1] == "pack":
             ref[...] = jnp.zeros_like(ref)
-
-    blocks = [(lo, lo + 256) for lo in range(0, full, 256)] + [(full, hidden)]
-    step_rows = rows // 2
-
-    def products(lo, hi, r):
-        if lo < full:
-            return nt(xv[r, :], wgv[lo:hi, :]), nt(xv[r, :], wuv[lo:hi, :]), nt(cv[r, :], wdv[lo:hi, :])
-        both = nt(xv[r, :], wrem[...])
-        return both[:, 0:rest], both[:, LANE : LANE + rest], nt(cv[r, :], wdv[lo:hi, :])
-
-    def terms(lo, hi, r, gate_pre, up_pre, back):
-        gelu_value, gelu_slope = gelu_pair(gate_pre)
-        hid[r, lo:hi] = (gelu_value * up_pre).astype(BF16)
-        dg[r, lo:hi] = (back * up_pre * gelu_slope).astype(BF16)
-        du[r, lo:hi] = (back * gelu_value).astype(BF16)
-
-    row_blocks = [slice(lo, lo + step_rows) for lo in range(0, rows, step_rows)]
-    taken = 0
-    before = None
     for i, (lo, hi) in enumerate(blocks):
-        count = 5 if i == 0 else 3
+        count = 4 if i == 0 else 3
         for load in loads[taken : taken + count]:
             load.wait()
         taken += count
         now = []
         for j, r in enumerate(row_blocks):
-            now.append(products(lo, hi, r))
-            if before is not None:
-                terms(*blocks[i - 1], r, *before[j])
+            parts = []
+            third = (r.stop - r.start) // 3
+            for k, part in enumerate(products(lo, hi, r)):
+                parts.append(part)
+                if before is None:
+                    turn(3 * j + k)
+                else:
+                    sub = slice(k * third, (k + 1) * third)
+                    rows_now = slice(r.start + sub.start, r.start + sub.stop)
+                    terms(*blocks[i - 1], rows_now, *(value[sub] for value in before[j]))
+            now.append(parts)
         before = now
     for load in loads[taken:]:
         load.wait()
 
-    slot_rows = [slice(e * seq, (e + 1) * seq) for e in range(SLOTS)]
-    gram_x = [nt(xv[r, :], xv[r, :]) for r in slot_rows]
     gram_c = [nt(cv[r, :], cv[r, :]) for r in slot_rows]
     for j, r in enumerate(row_blocks):
         terms(*blocks[-1], r, *before[j])
@@ -268,21 +303,6 @@
         remote(nrm_send, nrm_recv.at[k - 1], nrm_ssem.at[k - 1], nrm_rsem.at[k - 1], f_dev(k))
         for k in range(1, n_f)
     ]
-
-    def reorder(dst):
-        for ox in range(NX):
-            for oz in range(NZ):
-                src_at = OWN * (NZ * ox + oz)
-                dst_at = OWN * (NX * oz + ox)
-                dst[dst_at : dst_at + OWN, :] = stage[src_at : src_at + OWN, :]
-
-    turned = xv[...].T
-    xt[...] = turned
-    stage[...] = turned.astype(F32)
-    reorder(perm)
-    xt_z[...] = perm[...].astype(BF16)
-    stage[...] = cv[...].T.astype(F32)
-    reorder(perm)
 
     for copy in norm_copies:
         copy.wait_recv()
@@ -459,9 +479,10 @@
     vmem = pl.BlockSpec(memory_space=pltpu.VMEM)
     dma = pltpu.SemaphoreType.DMA
     out = jax.ShapeDtypeStruct((OWN, hidden), F32)
+    held = pltpu.VMEM((OWN, hidden), F32)
     gate, up, down = pl.pallas_call(
         functools.partial(kernel, n_f, seq, hidden, bound),
-        out_shape=(out, out, out),
+        out_shape=(held, held, held),
         in_specs=[pl.BlockSpec(memory_space=pltpu.SMEM)] + [any_spec] * 5,
         out_specs=(vmem, vmem, vmem),
         scratch_shapes=[
@@ -474,6 +495,7 @@
             pltpu.VMEM((rows, HP), BF16),
             pltpu.VMEM((rows, HP), BF16),
             pltpu.VMEM((rows, HP), BF16),
+            pltpu.VMEM((SLOTS, seq, seq), F32),
             pltpu.VMEM((D, rows), F32),
             pltpu.VMEM((D, rows), F32),
             pltpu.VMEM((D, rows), BF16),
@@ -498,6 +520,7 @@
         out_shape=(out, out, out),
         in_specs=[vmem] * 6,
         out_specs=(vmem, vmem, vmem),
+        compiler_params=pltpu.CompilerParams(vmem_limit_bytes=4 * 1024 * 1024),
     )(gate, up, down, noise_gate, noise_up, noise_down.T)
     return gate, up, down.T
 

time: 69.8 us -> 67.2 us (0.963)
  Pallas kernels: 68.4 us -> 65.8 us
    pallas_call x1, Pallas kernels: 66.4 us -> 65 us  [per_device(): pl.pallas_call(functools.partial(kernel, n_f, seq, hidden, bound), out_sh...]
    pallas_call x1, Pallas kernels: 2.01 us -> 0.82 us  [per_device(): pl.pallas_call(add_noise, out_shape=(out, out, out), in_specs=[vmem] * 6,...]
where the time goes in v3:
time: 67.2 us; the launch traced here: 67.1 us
  Pallas kernels  65.8 us (98%)
  between operations  1.33 us (2%)
    pallas_call x1, Pallas kernels, per_device(): pl.pallas_call(functools.partial(kernel, n_f, seq, hidden, bound), out_sh...  65 us

profile of v3, /device:TPU:2, one launch (start us, length us, event | category | flops | bytes accessed | tf_op | source)
XLA Modules:
  0.0 67.1 jit_solution(3968073864448555165)
XLA Ops:
  1.3 0.0 copy-start
  1.3 0.0 copy-start.1
  1.3 0.0 copy-start.2
  1.3 65.0 %shard_map.112 = (f32[36,864]{1,0:T(8,128)S(1)}, f32[36,864]{1,0:T(8,128)S(1)}, f32[36,864]{1,0:T(8,128)S(1)}) custom-call(s32[1]{0:T(128)S(6)} %copy.12.live_ref, bf16[768,1152]{1,0:T(8,128)(2,1)} %x_hbm.1, bf16[768,1152]{1,0:T(8,128)(2,1)} %c_hbm.1, bf16[864,1152]{1,0:T(8,128)(2,1)} %bitcast.5, bf16[864,1152]{1,0:T(8,128)(2,1)} %bitcast.6, ...), custom_call_target="tpu_custom_call" | custom-call | tf_op jit(solution)/shard_map/pallas_call | solution.py:483
  66.3 0.0 copy-done
  66.3 0.0 copy-done.1
  66.3 0.0 copy-done.2
  66.3 0.8 %shard_map.113 = (f32[36,864]{1,0:T(8,128)}, f32[36,864]{1,0:T(8,128)}, f32[36,864]{1,0:T(8,128)}) custom-call(f32[36,864]{1,0:T(8,128)S(1)} %get-tuple-element.9.gate_ref, f32[36,864]{1,0:T(8,128)S(1)} %get-tuple-element.10.up_ref, f32[36,864]{1,0:T(8,128)S(1)} %get-tuple-element.11.down_ref, f32[36,864]{1,0:T(8,128)S(1)} %copy-done, ...), custom_call_target="tpu_custom_call" | custom-call | tf_op jit(solution)/shard_map/pallas_call | solution.py:518
Async XLA Ops:
  1.3 65.0 %copy-start = (f32[36,864]{1,0:T(8,128)S(1)}, f32[36,864]{1,0:T(8,128)}, u32[]{:S(2)}) copy-start(f32[36,864]{1,0:T(8,128)} %ng_ref.1) | copy-start | bytes 373252
  1.3 65.0 %copy-start.1 = (f32[36,864]{1,0:T(8,128)S(1)}, f32[36,864]{1,0:T(8,128)}, u32[]{:S(2)}) copy-start(f32[36,864]{1,0:T(8,128)} %nu_ref.1) | copy-start | bytes 373252
  1.3 65.0 %copy-start.2 = (f32[864,36]{0,1:T(8,128)S(1)}, f32[864,36]{0,1:T(8,128)}, u32[]{:S(2)}) copy-start(f32[864,36]{0,1:T(8,128)} %param.17) | copy-start | bytes 373252

commit v4 on v3

--- a/solution.py
+++ b/solution.py
@@ -25,19 +25,24 @@
 gelu_scale = 0.7978845608028654
 gelu_cube = 0.044715
 
+HIDDEN = FF // 8
 HP = 896
+REST = HIDDEN % LANE
 GROUPS = (
-    ("z", ((("up", 512, 896),), (("down", 0, 256),)), "direct"),
-    ("x", ((("gate", 0, 512),), (("gate", 512, 896), ("up", 0, 128),)), "chain"),
-    ("z", ((("down", 256, 512),), (("down", 512, 896),)), "direct"),
-    ("x", ((("up", 128, 384),), (("up", 384, 512),)), "tree"),
+    ("x", ((("gate", 0, 256),), (("gate", 640, 896),)), "chain"),
+    ("x", ((("gate", 256, 512),), (("up", 640, 896),)), "chain"),
+    ("x", ((("gate", 512, 640),), (("up", 0, 128),)), "tree"),
+    ("x", ((("up", 128, 256),), (("up", 256, 384),)), "tree"),
+    ("z", ((("down", 0, 640),), (("up", 384, 640), ("down", 640, 896),)), "direct"),
 )
 ORDER = (
-    (2, 1, 0), (1, 1, 0), (2, 1, 1), (0, 1, 0), (0, 1, 1), (1, 1, 1), (2, 1, 2), (2, 1, 3),
-    (0, 1, 2), (1, 1, 2), (0, 1, 3), (2, 1, 4), (2, 1, 5), (3, 1, 0), (0, 1, 4), (3, 1, 1),
-    (0, 1, 5), (1, 0, 0), (2, 1, 6), (1, 2, 0), (3, 1, 2), (1, 2, 1), (0, 1, 6), (2, 0, 0),
-    (2, 2, 0), (1, 2, 2), (1, 2, 3), (3, 0, 0), (3, 2, 0), (3, 2, 1), (0, 0, 0), (0, 2, 0),
-    (1, 2, 4), (1, 2, 5), (2, 3, 0), (3, 2, 2), (1, 2, 6), (0, 3, 0), (3, 3, 0), (1, 3, 0),
+    (0, 1, 0), (4, 1, 0), (0, 1, 1), (4, 1, 1), (1, 1, 0), (4, 1, 2), (0, 1, 2), (4, 1, 3),
+    (1, 1, 1), (4, 1, 4), (1, 1, 2), (0, 0, 0), (0, 2, 0), (0, 2, 1), (3, 1, 0), (4, 1, 5),
+    (3, 1, 1), (2, 1, 0), (1, 0, 0), (1, 2, 0), (1, 2, 1), (2, 1, 1), (0, 2, 2), (0, 2, 3),
+    (4, 1, 6), (3, 1, 2), (2, 1, 2), (1, 2, 2), (1, 2, 3), (0, 2, 4), (0, 2, 5), (3, 0, 0),
+    (3, 2, 0), (3, 2, 1), (4, 0, 0), (2, 0, 0), (2, 2, 0), (2, 2, 1), (4, 2, 0), (1, 2, 4),
+    (1, 2, 5), (0, 2, 6), (3, 2, 2), (2, 2, 2), (1, 2, 6), (0, 3, 0), (3, 3, 0), (4, 3, 0),
+    (1, 3, 0), (2, 3, 0),
 )
 RING = {"x": NX, "z": NZ}
 
@@ -124,23 +129,65 @@
     return sends
 
 
+def tile_rows(axis, half):
+    rows = XROWS if axis == "x" else ZROWS
+    return [
+        rows if at + LANE <= HIDDEN else rows * 7 // 9 for _, lo, hi in half for at in range(lo, hi, LANE)
+    ]
+
+
+def blocks_of(g, phase, halves):
+    axis, all_halves, _ = GROUPS[g]
+    if phase == 1:
+        (h,) = halves
+        return [((h, t), n) for t, n in enumerate(tile_rows(axis, all_halves[h]))]
+    packed = packed_rows(g)
+    return [((h,), packed[h]) for h in halves]
+
+
 def scratch_plan():
     shapes = {}
     for g, (axis, halves, _) in enumerate(GROUPS):
         rows = XROWS if axis == "x" else ZROWS
         other = NZ if axis == "x" else NX
-        first = RING[axis] - 1
         for h, half in enumerate(halves):
-            width = width_of(half)
-            shapes[g, h, "s1"] = ((first, rows, width), BF16)
-            shapes[g, h, "r1"] = ((first, rows, width), BF16)
-            shapes[g, h, "sum"] = ((rows, width), F32)
-        packed = packed_rows(g)
-        shapes[g, "pack"] = ((other * sum(packed), LANE), F32)
-        total = sum(packed[h] for send in plan()[g, 2][1] for h in send[2])
-        shapes[g, "s2"] = ((total, LANE), BF16)
-        shapes[g, "r2"] = ((total, LANE), BF16)
+            shapes[g, h, "sum"] = ((rows, width_of(half)), F32)
+        shapes[g, "pack"] = ((other * sum(packed_rows(g)), LANE), F32)
+        for phase in (1, 2):
+            total = sum(n for send in plan()[g, phase][1] for _, n in blocks_of(g, phase, send[2]))
+            shapes[g, f"s{phase}"] = ((total, LANE), BF16)
+            shapes[g, f"r{phase}"] = ((total, LANE), BF16)
     return shapes
+
+
+def lane_mask(shape, lo, hi):
+    lane = lax.broadcasted_iota(jnp.int32, shape, 1)
+    return (lane >= lo) & (lane < hi)
+
+
+def fold(tile):
+    rows = tile.shape[0]
+    main = rows * 7 // 9
+    rest = rows - main
+    left = tile[main:rows, :]
+    parts = []
+    for j in range(3):
+        moved = pltpu.roll(left, REST - 32 * j, 1)
+        own = tile[rest * j : rest * (j + 1), :]
+        parts.append(jnp.where(lane_mask(own.shape, REST, LANE), moved, own))
+    parts.append(tile[3 * rest : main, :])
+    return jnp.concatenate(parts, axis=0)
+
+
+def unfold(tile):
+    main = tile.shape[0]
+    rows = main * 9 // 7
+    rest = rows - main
+    left = jnp.zeros((rest, LANE), F32)
+    for j in range(3):
+        moved = pltpu.roll(tile[rest * j : rest * (j + 1), :], 32 * j + LANE - REST, 1)
+        left = jnp.where(lane_mask(left.shape, 32 * j, 32 * (j + 1)), moved, left)
+    return jnp.concatenate([tile, left], axis=0)
 
 
 def total_sends():
@@ -345,77 +392,67 @@
         for src, lo, hi in halves[h]:
             right = right_side(src, lo, hi)
             parts.append(nn(left_side(axis, src, k), right))
-        return parts[0] if len(parts) == 1 else jnp.concatenate(parts, axis=1)
+        tiles = [part[:, at : at + LANE] for part in parts for at in range(0, part.shape[1], LANE)]
+        return [
+            tile if n == tile.shape[0] else fold(tile) for tile, n in zip(tiles, tile_rows(axis, halves[h]))
+        ]
 
     routes = plan()
     copies = {}
     spot = {}
     numbers = {}
     for (g, phase), (ring, sends) in routes.items():
-        used = [0, 0]
         row = 0
-        packed = packed_rows(g)
-        for i, (step, way, halves, owner, target, adds) in enumerate(sends):
+        for i, (_, _, halves, _, _, _) in enumerate(sends):
             numbers[g, phase, i] = len(numbers)
-            if phase == 1:
-                spot[g, phase, i] = (used[halves[0]],)
-                used[halves[0]] += 1
-            else:
-                n = sum(packed[h] for h in halves)
-                spot[g, phase, i] = (row, n)
-                row += n
-
-    def received(g, phase, i, h):
-        if phase == 1:
-            return buf[g, h, "r1"][spot[g, phase, i][0]].astype(F32)
+            n = sum(n for _, n in blocks_of(g, phase, halves))
+            spot[g, phase, i] = (row, n)
+            row += n
+
+    def received(g, phase, i):
         row, _ = spot[g, phase, i]
-        packed = packed_rows(g)
-        for half in routes[g, phase][1][i][2]:
-            if half == h:
-                return buf[g, "r2"][row : row + packed[h], :].astype(F32)
-            row += packed[half]
+        found = {}
+        for key, n in blocks_of(g, phase, routes[g, phase][1][i][2]):
+            found[key] = slice(row, row + n)
+            row += n
+        return {key: buf[g, f"r{phase}"][r, :].astype(F32) for key, r in found.items()}
 
     def send(g, phase, step):
         ring, sends = routes[g, phase]
-        packed = packed_rows(g)
         for i, (at_step, way, halves, owner, target, adds) in enumerate(sends):
             if at_step != step:
                 continue
-            values = []
-            for h in halves:
-                if phase == 1:
-                    value = product(g, h, owner)
-                else:
-                    n = sum(packed)
+            blocks = blocks_of(g, phase, halves)
+            if phase == 1:
+                values = product(g, halves[0], owner)
+            else:
+                packed = packed_rows(g)
+                n = sum(packed)
+                values = []
+                for h in halves:
                     first = pl.multiple_of(at(ring, owner) * n, n) + (packed[0] if h else 0)
-                    value = buf[g, "pack"][pl.ds(pl.multiple_of(first, 16), packed[h]), :]
-                values.append(value)
+                    values.append(buf[g, "pack"][pl.ds(pl.multiple_of(first, 16), packed[h]), :])
             for j in adds:
                 copies[g, phase, j].wait_recv()
-                for k, h in enumerate(halves):
-                    if h in sends[j][2]:
-                        values[k] = values[k] + received(g, phase, j, h)
-            if phase == 1:
-                h, slot = halves[0], spot[g, phase, i][0]
-                src, dst = buf[g, h, "s1"].at[slot], buf[g, h, "r1"].at[slot]
-                src[...] = values[0].astype(BF16)
-            else:
-                row, n = spot[g, phase, i]
-                src, dst = buf[g, "s2"].at[pl.ds(row, n), :], buf[g, "r2"].at[pl.ds(row, n), :]
-                for k, h in enumerate(halves):
-                    buf[g, "s2"][row : row + packed[h], :] = values[k].astype(BF16)
-                    row += packed[h]
+                came = received(g, phase, j)
+                values = [v + came[key] if key in came else v for v, (key, _) in zip(values, blocks)]
+            row, n = spot[g, phase, i]
+            src, dst = (buf[g, f"{side}{phase}"].at[pl.ds(row, n), :] for side in "sr")
+            for value, (_, rows_now) in zip(values, blocks):
+                buf[g, f"s{phase}"][row : row + rows_now, :] = value.astype(BF16)
+                row += rows_now
             number = numbers[g, phase, i]
             copies[g, phase, i] = remote(src, dst, ssem.at[number], rsem.at[number], neighbour(ring, target))
 
-    def arrived(g, phase, h, value):
+    def arrived(g, phase, h, values):
         for i, (_, _, halves, owner, target, _) in enumerate(routes[g, phase][1]):
             if owner == target and h in halves:
                 if (g, phase, i) not in waited:
                     waited.add((g, phase, i))
                     copies[g, phase, i].wait_recv()
-                value = value + received(g, phase, i, h)
-        return value
+                came = received(g, phase, i)
+                values = [v + came[key] for v, (key, _) in zip(values, blocks_of(g, phase, (h,)))]
+        return values
 
     waited = set()
 
@@ -424,7 +461,10 @@
         packed = packed_rows(g)
         for h, half in enumerate(halves):
             full_sum, pack = buf[g, h, "sum"], buf[g, "pack"]
-            full_sum[...] = arrived(g, 1, h, product(g, h, 0))
+            for t, tile in enumerate(arrived(g, 1, h, product(g, h, 0))):
+                if tile.shape[0] < full_sum.shape[0]:
+                    tile = unfold(tile)
+                full_sum[:, LANE * t : LANE * t + LANE] = tile
             for o in range(NZ if axis == "x" else NX):
                 for t in range(width_of(half) // LANE):
                     to = o * sum(packed) + (packed[0] if h else 0) + OWN * t
@@ -441,8 +481,7 @@
         for h, half in enumerate(halves):
             row = packed[0] if h else 0
             own = pack[pl.ds(pl.multiple_of(pl.multiple_of(base, n) + row, 16), packed[h]), :]
-            buf_sum = fin.at[pl.ds(row, packed[h]), :]
-            buf_sum[...] = arrived(g, 2, h, own)
+            (fin[row : row + packed[h], :],) = arrived(g, 2, h, [own])
             for src, lo, hi in half:
                 for start in range(lo, hi, LANE):
                     width = min(LANE, hidden - start)

time: 67.2 us -> 66.8 us (level)
  no operation moved by 1% of the time
where the time goes in v4:
time: 66.8 us; the launch traced here: 66.7 us
  Pallas kernels  65.4 us (98%)
  between operations  1.33 us (2%)
    pallas_call x1, Pallas kernels, per_device(): pl.pallas_call(functools.partial(kernel, n_f, seq, hidden, bound), out_sh...  64.5 us

profile of v4, /device:TPU:2, one launch (start us, length us, event | category | flops | bytes accessed | tf_op | source)
XLA Modules:
  0.0 66.7 jit_solution(922661214724106536)
XLA Ops:
  1.3 0.0 copy-start
  1.3 0.0 copy-start.1
  1.3 0.0 copy-start.2
  1.3 64.5 %shard_map.112 = (f32[36,864]{1,0:T(8,128)S(1)}, f32[36,864]{1,0:T(8,128)S(1)}, f32[36,864]{1,0:T(8,128)S(1)}) custom-call(s32[1]{0:T(128)S(6)} %copy.12.live_ref, bf16[768,1152]{1,0:T(8,128)(2,1)} %x_hbm.1, bf16[768,1152]{1,0:T(8,128)(2,1)} %c_hbm.1, bf16[864,1152]{1,0:T(8,128)(2,1)} %bitcast.5, bf16[864,1152]{1,0:T(8,128)(2,1)} %bitcast.6, ...), custom_call_target="tpu_custom_call" | custom-call | tf_op jit(solution)/shard_map/pallas_call | solution.py:522
  65.9 0.0 copy-done
  65.9 0.0 copy-done.1
  65.9 0.0 copy-done.2
  65.9 0.8 %shard_map.113 = (f32[36,864]{1,0:T(8,128)}, f32[36,864]{1,0:T(8,128)}, f32[36,864]{1,0:T(8,128)}) custom-call(f32[36,864]{1,0:T(8,128)S(1)} %get-tuple-element.9.gate_ref, f32[36,864]{1,0:T(8,128)S(1)} %get-tuple-element.10.up_ref, f32[36,864]{1,0:T(8,128)S(1)} %get-tuple-element.11.down_ref, f32[36,864]{1,0:T(8,128)S(1)} %copy-done, ...), custom_call_target="tpu_custom_call" | custom-call | tf_op jit(solution)/shard_map/pallas_call | solution.py:557
Async XLA Ops:
  1.3 64.6 %copy-start = (f32[36,864]{1,0:T(8,128)S(1)}, f32[36,864]{1,0:T(8,128)}, u32[]{:S(2)}) copy-start(f32[36,864]{1,0:T(8,128)} %ng_ref.1) | copy-start | bytes 373252
  1.3 64.6 %copy-start.1 = (f32[36,864]{1,0:T(8,128)S(1)}, f32[36,864]{1,0:T(8,128)}, u32[]{:S(2)}) copy-start(f32[36,864]{1,0:T(8,128)} %nu_ref.1) | copy-start | bytes 373252
  1.3 64.6 %copy-start.2 = (f32[864,36]{0,1:T(8,128)S(1)}, f32[864,36]{0,1:T(8,128)}, u32[]{:S(2)}) copy-start(f32[864,36]{0,1:T(8,128)} %param.17) | copy-start | bytes 373252

commit v5 on v4

--- a/solution.py
+++ b/solution.py
@@ -117,7 +117,8 @@
 
 
 def packed_rows(g):
-    return [pad16(OWN * width_of(half) // LANE) for half in GROUPS[g][1]]
+    n = pad16(OWN * sum(width_of(half) for half in GROUPS[g][1]) // LANE)
+    return [n // 32 * 16, n - n // 32 * 16]
 
 
 def plan():
@@ -294,6 +295,7 @@
     slot_rows = [slice(e * seq, (e + 1) * seq) for e in range(SLOTS)]
     for e, r in enumerate(slot_rows):
         gram_x[e] = nt(xv[r, :], xv[r, :])
+    nrm_send[...] = jnp.zeros_like(nrm_send)
     for ref in (hid, dg, du):
         ref[:, HP - LANE : HP] = jnp.zeros((rows, LANE), BF16)
     wrem[rest:LANE, :] = jnp.zeros((LANE - rest, D), BF16)
@@ -332,7 +334,7 @@
         part = prod[:, 0:LANE]
         for lo in range(LANE, seq, LANE):
             part = part + prod[:, lo : lo + LANE]
-        nrm_send[8 * e : 8 * e + 8, :] = part.reshape(seq // 8, 8, LANE).sum(axis=0)
+        nrm_send[e : e + 1, :] = jnp.sum(part, axis=0, keepdims=True)
 
     pl.semaphore_wait(barrier, len(peers))
 
@@ -351,19 +353,37 @@
         for k in range(1, n_f)
     ]
 
+    matrix = {"gate": dg, "up": du, "down": hid}
+    routes = plan()
+    slot_products = {}
+    for first in ("x", "z"):
+        g = next(g for g, phase, _ in ORDER if phase == 1 and GROUPS[g][0] == first)
+        for step, _, (h,), owner, _, _ in routes[g, 1][1]:
+            if step > 0:
+                continue
+            n = XROWS if first == "x" else ZROWS
+            r = pl.ds(pl.multiple_of(at(first, owner) * n, n), n)
+            parts = []
+            for src, lo, hi in GROUPS[g][1][h]:
+                for e in range(SLOTS):
+                    c = slice(e * seq, (e + 1) * seq)
+                    if src == "down":
+                        left = perm[r, c].astype(BF16)
+                    else:
+                        left = xt[r, c] if first == "x" else xt_z[r, c]
+                    parts.append(nn(left, matrix[src][c, lo:hi]))
+            slot_products[g, h, owner] = parts
+
     for copy in norm_copies:
         copy.wait_recv()
     total = nrm_send[...]
     for k in range(n_f - 1):
         total = total + nrm_recv[k]
     live = live_ref[0]
-    factors = []
-    for e in range(SLOTS):
-        squared = jnp.sum(total[8 * e : 8 * e + 8, :], axis=(0, 1), keepdims=True)
-        is_live = jnp.where(e < live, 1.0, 0.0).astype(F32)
-        factors.append(is_live * bound / jnp.maximum(jnp.sqrt(jnp.maximum(squared, 0.0)), bound))
-
-    matrix = {"gate": dg, "up": du, "down": hid}
+    squared = jnp.sum(total, axis=1, keepdims=True)
+    is_live = jnp.where(lax.broadcasted_iota(jnp.int32, squared.shape, 0) < live, 1.0, 0.0).astype(F32)
+    factor = is_live * bound / jnp.maximum(jnp.sqrt(jnp.maximum(squared, 0.0)), bound)
+    factors = [factor[e : e + 1, :] for e in range(SLOTS)]
     scaled = set()
 
     def right_side(src, lo, hi):
@@ -389,15 +409,18 @@
     def product(g, h, k):
         axis, halves, _ = GROUPS[g]
         parts = []
-        for src, lo, hi in halves[h]:
-            right = right_side(src, lo, hi)
-            parts.append(nn(left_side(axis, src, k), right))
+        early = slot_products.get((g, h, k))
+        for i, (src, lo, hi) in enumerate(halves[h]):
+            if early is None:
+                right = right_side(src, lo, hi)
+                parts.append(nn(left_side(axis, src, k), right))
+            else:
+                parts.append(sum(early[i * SLOTS + e] * factors[e] for e in range(SLOTS)))
         tiles = [part[:, at : at + LANE] for part in parts for at in range(0, part.shape[1], LANE)]
         return [
             tile if n == tile.shape[0] else fold(tile) for tile, n in zip(tiles, tile_rows(axis, halves[h]))
         ]
 
-    routes = plan()
     copies = {}
     spot = {}
     numbers = {}
@@ -459,6 +482,7 @@
     def close_first(g):
         axis, halves, _ = GROUPS[g]
         packed = packed_rows(g)
+        first = 0
         for h, half in enumerate(halves):
             full_sum, pack = buf[g, h, "sum"], buf[g, "pack"]
             for t, tile in enumerate(arrived(g, 1, h, product(g, h, 0))):
@@ -467,8 +491,9 @@
                 full_sum[:, LANE * t : LANE * t + LANE] = tile
             for o in range(NZ if axis == "x" else NX):
                 for t in range(width_of(half) // LANE):
-                    to = o * sum(packed) + (packed[0] if h else 0) + OWN * t
+                    to = o * sum(packed) + OWN * (first + t)
                     pack[to : to + OWN, :] = full_sum[OWN * o : OWN * o + OWN, LANE * t : LANE * t + LANE]
+            first += width_of(half) // LANE
 
     out = {"gate": gate_ref, "up": up_ref, "down": down_ref}
 
@@ -478,15 +503,16 @@
         n = sum(packed)
         pack = buf[g, "pack"]
         base = mine["z" if axis == "x" else "x"] * n
-        for h, half in enumerate(halves):
+        for h in range(2):
             row = packed[0] if h else 0
             own = pack[pl.ds(pl.multiple_of(pl.multiple_of(base, n) + row, 16), packed[h]), :]
             (fin[row : row + packed[h], :],) = arrived(g, 2, h, [own])
-            for src, lo, hi in half:
-                for start in range(lo, hi, LANE):
-                    width = min(LANE, hidden - start)
-                    out[src][:, start : start + width] = fin[row : row + OWN, 0:width]
-                    row += OWN
+        row = 0
+        for src, lo, hi in halves[0] + halves[1]:
+            for start in range(lo, hi, LANE):
+                width = min(LANE, hidden - start)
+                out[src][:, start : start + width] = fin[row : row + OWN, 0:width]
+                row += OWN
 
     for g, phase, step in ORDER:
         if phase == 0:
@@ -540,8 +566,8 @@
             pltpu.VMEM((D, rows), BF16),
             pltpu.VMEM((D, rows), BF16),
             pltpu.VMEM((D, rows), BF16),
-            pltpu.VMEM((8 * SLOTS, LANE), F32),
-            pltpu.VMEM((max(n_f - 1, 1), 8 * SLOTS, LANE), F32),
+            pltpu.VMEM((8, LANE), F32),
+            pltpu.VMEM((max(n_f - 1, 1), 8, LANE), F32),
             pltpu.VMEM((max(sum(packed_rows(g)) for g in range(len(GROUPS))), LANE), F32),
             dma((2 + 3 * (full // 256) + 3,)),
             dma((max(n_f - 1, 1),)),

time: 66.8 us -> 64.8 us (0.970)
  Pallas kernels: 65.4 us -> 63.1 us
    pallas_call x1, Pallas kernels: 64.5 us -> 62.2 us  [per_device(): pl.pallas_call(functools.partial(kernel, n_f, seq, hidden, bound), out_sh...]
where the time goes in v5:
time: 64.8 us; the launch traced here: 64.4 us
  Pallas kernels  63.1 us (97%)
  between operations  1.33 us (2%)
    pallas_call x1, Pallas kernels, per_device(): pl.pallas_call(functools.partial(kernel, n_f, seq, hidden, bound), out_sh...  62.2 us

profile of v5, /device:TPU:2, one launch (start us, length us, event | category | flops | bytes accessed | tf_op | source)
XLA Modules:
  0.0 64.4 jit_solution(8747877482544786917)
XLA Ops:
  1.3 0.0 copy-start
  1.3 0.0 copy-start.1
  1.3 0.0 copy-start.2
  1.3 62.2 %shard_map.112 = (f32[36,864]{1,0:T(8,128)S(1)}, f32[36,864]{1,0:T(8,128)S(1)}, f32[36,864]{1,0:T(8,128)S(1)}) custom-call(s32[1]{0:T(128)S(6)} %copy.12.live_ref, bf16[768,1152]{1,0:T(8,128)(2,1)} %x_hbm.1, bf16[768,1152]{1,0:T(8,128)(2,1)} %c_hbm.1, bf16[864,1152]{1,0:T(8,128)(2,1)} %bitcast.5, bf16[864,1152]{1,0:T(8,128)(2,1)} %bitcast.6, ...), custom_call_target="tpu_custom_call" | custom-call | tf_op jit(solution)/shard_map/pallas_call | solution.py:548
  63.6 0.0 copy-done
  63.6 0.0 copy-done.1
  63.6 0.0 copy-done.2
  63.6 0.8 %shard_map.113 = (f32[36,864]{1,0:T(8,128)}, f32[36,864]{1,0:T(8,128)}, f32[36,864]{1,0:T(8,128)}) custom-call(f32[36,864]{1,0:T(8,128)S(1)} %get-tuple-element.9.gate_ref, f32[36,864]{1,0:T(8,128)S(1)} %get-tuple-element.10.up_ref, f32[36,864]{1,0:T(8,128)S(1)} %get-tuple-element.11.down_ref, f32[36,864]{1,0:T(8,128)S(1)} %copy-done, ...), custom_call_target="tpu_custom_call" | custom-call | tf_op jit(solution)/shard_map/pallas_call | solution.py:583
Async XLA Ops:
  1.3 62.3 %copy-start = (f32[36,864]{1,0:T(8,128)S(1)}, f32[36,864]{1,0:T(8,128)}, u32[]{:S(2)}) copy-start(f32[36,864]{1,0:T(8,128)} %ng_ref.1) | copy-start | bytes 373252
  1.3 62.3 %copy-start.1 = (f32[36,864]{1,0:T(8,128)S(1)}, f32[36,864]{1,0:T(8,128)}, u32[]{:S(2)}) copy-start(f32[36,864]{1,0:T(8,128)} %nu_ref.1) | copy-start | bytes 373252
  1.3 62.3 %copy-start.2 = (f32[864,36]{0,1:T(8,128)S(1)}, f32[864,36]{0,1:T(8,128)}, u32[]{:S(2)}) copy-start(f32[864,36]{0,1:T(8,128)} %param.17) | copy-start | bytes 373252

commit v6 on v5

--- a/solution.py
+++ b/solution.py
@@ -36,7 +36,7 @@
     ("z", ((("down", 0, 640),), (("up", 384, 640), ("down", 640, 896),)), "direct"),
 )
 ORDER = (
-    (0, 1, 0), (4, 1, 0), (0, 1, 1), (4, 1, 1), (1, 1, 0), (4, 1, 2), (0, 1, 2), (4, 1, 3),
+    (4, 1, 0), (0, 1, 0), (0, 1, 1), (4, 1, 1), (1, 1, 0), (4, 1, 2), (0, 1, 2), (4, 1, 3),
     (1, 1, 1), (4, 1, 4), (1, 1, 2), (0, 0, 0), (0, 2, 0), (0, 2, 1), (3, 1, 0), (4, 1, 5),
     (3, 1, 1), (2, 1, 0), (1, 0, 0), (1, 2, 0), (1, 2, 1), (2, 1, 1), (0, 2, 2), (0, 2, 3),
     (4, 1, 6), (3, 1, 2), (2, 1, 2), (1, 2, 2), (1, 2, 3), (0, 2, 4), (0, 2, 5), (3, 0, 0),
@@ -442,10 +442,10 @@
 
     def send(g, phase, step):
         ring, sends = routes[g, phase]
+        own = {}
         for i, (at_step, way, halves, owner, target, adds) in enumerate(sends):
             if at_step != step:
                 continue
-            blocks = blocks_of(g, phase, halves)
             if phase == 1:
                 values = product(g, halves[0], owner)
             else:
@@ -455,6 +455,10 @@
                 for h in halves:
                     first = pl.multiple_of(at(ring, owner) * n, n) + (packed[0] if h else 0)
                     values.append(buf[g, "pack"][pl.ds(pl.multiple_of(first, 16), packed[h]), :])
+            own[i] = values
+        for i, values in own.items():
+            _, _, halves, _, target, adds = sends[i]
+            blocks = blocks_of(g, phase, halves)
             for j in adds:
                 copies[g, phase, j].wait_recv()
                 came = received(g, phase, j)

time: 64.8 us -> 65 us (level)
  no operation moved by 1% of the time
where the time goes in v6:
time: 65 us; the launch traced here: 64.3 us
  Pallas kernels  62.9 us (97%)
  between operations  1.33 us (2%)
    pallas_call x1, Pallas kernels, per_device(): pl.pallas_call(functools.partial(kernel, n_f, seq, hidden, bound), out_sh...  62.1 us

profile of v6, /device:TPU:2, one launch (start us, length us, event | category | flops | bytes accessed | tf_op | source)
XLA Modules:
  0.0 64.3 jit_solution(1630193074722417847)
XLA Ops:
  1.3 0.0 copy-start
  1.3 0.0 copy-start.1
  1.3 0.0 copy-start.2
  1.3 62.1 %shard_map.112 = (f32[36,864]{1,0:T(8,128)S(1)}, f32[36,864]{1,0:T(8,128)S(1)}, f32[36,864]{1,0:T(8,128)S(1)}) custom-call(s32[1]{0:T(128)S(6)} %copy.12.live_ref, bf16[768,1152]{1,0:T(8,128)(2,1)} %x_hbm.1, bf16[768,1152]{1,0:T(8,128)(2,1)} %c_hbm.1, bf16[864,1152]{1,0:T(8,128)(2,1)} %bitcast.5, bf16[864,1152]{1,0:T(8,128)(2,1)} %bitcast.6, ...), custom_call_target="tpu_custom_call" | custom-call | tf_op jit(solution)/shard_map/pallas_call | solution.py:552
  63.4 0.0 copy-done
  63.5 0.0 copy-done.1
  63.5 0.0 copy-done.2
  63.5 0.8 %shard_map.113 = (f32[36,864]{1,0:T(8,128)}, f32[36,864]{1,0:T(8,128)}, f32[36,864]{1,0:T(8,128)}) custom-call(f32[36,864]{1,0:T(8,128)S(1)} %get-tuple-element.9.gate_ref, f32[36,864]{1,0:T(8,128)S(1)} %get-tuple-element.10.up_ref, f32[36,864]{1,0:T(8,128)S(1)} %get-tuple-element.11.down_ref, f32[36,864]{1,0:T(8,128)S(1)} %copy-done, ...), custom_call_target="tpu_custom_call" | custom-call | tf_op jit(solution)/shard_map/pallas_call | solution.py:587
Async XLA Ops:
  1.3 62.2 %copy-start = (f32[36,864]{1,0:T(8,128)S(1)}, f32[36,864]{1,0:T(8,128)}, u32[]{:S(2)}) copy-start(f32[36,864]{1,0:T(8,128)} %ng_ref.1) | copy-start | bytes 373252
  1.3 62.2 %copy-start.1 = (f32[36,864]{1,0:T(8,128)S(1)}, f32[36,864]{1,0:T(8,128)}, u32[]{:S(2)}) copy-start(f32[36,864]{1,0:T(8,128)} %nu_ref.1) | copy-start | bytes 373252
  1.3 62.2 %copy-start.2 = (f32[864,36]{0,1:T(8,128)S(1)}, f32[864,36]{0,1:T(8,128)}, u32[]{:S(2)}) copy-start(f32[864,36]{0,1:T(8,128)} %param.17) | copy-start | bytes 373252
